TPU v7x, 128 devices: a whole 4x4x4 slice. The times are simulated.
128 devices in a mesh: row: 8 (over z, core), col: 16 (over x, y).
Axes of the slice: x: 4, y: 4, z: 4, core: 2. Of those that a mesh axis runs over, the one named last changes fastest.
Arguments:
- aux_ints: bfloat16 [512, 1024, 1024], P(('row', 'col')), may hold values from -4 to 4
- density: bfloat16 [1024, 1024], P(('row', 'col')), may hold values from -0.1875 to 0.1875
- pattern: int32 [512, 8, 8], P(('row', 'col')), may hold values from 0 to 1, as said below
- block_sizes: int32 [8], replicated, may hold values from 96 to 128
Outputs:
- exchange_k: float32 [1024, 1024], P('row', 'col')
Inputs may be any that keep to these rules, and one draw needn't show every extreme that they name: pattern[P, a, b] is 1 where both blocks a and b lie within a reach of the block of aux function P, else 0; every aux function has at least its own diagonal block.
All inputs are finite; a program needn't handle non-finite values.
Results may differ from a plain program's by a relative error of at most 0.0029.
Values may be sent and summed in bfloat16 or wider, within the bound.
No kernel may reach another device: no remote copies, remote signals or barrier semaphores. Data moves between devices by JAX's collectives and lax.ppermute only.
A program may use at most 128 MiB of HBM per device.

v0:
```python
import jax
import jax.numpy as jnp
from jax import lax
from jax.sharding import PartitionSpec as P


def mask_aux(aux_ints, pattern, block_sizes):
    aux_count, orbitals, _ = aux_ints.shape
    blocks = pattern.shape[1]
    block_width = orbitals // blocks
    inside = (
        jnp.arange(orbitals, dtype=jnp.int32) % block_width < jnp.repeat(block_sizes, block_width)
    ).astype(aux_ints.dtype)
    shaped = aux_ints.reshape(aux_count, blocks, block_width, blocks, block_width)
    shaped = shaped * pattern[:, :, None, :, None].astype(aux_ints.dtype)
    return (
        shaped.reshape(aux_count, orbitals, orbitals)
        * inside[None, :, None]
        * inside[None, None, :]
    )


def local(aux_ints, density, pattern, block_sizes):
    masked = mask_aux(aux_ints, pattern, block_sizes)
    whole_density = lax.all_gather(density, ("row", "col"), axis=0, tiled=True)
    coeff = jnp.einsum(
        "pmk,kn->pmn", masked, whole_density, preferred_element_type=jnp.float32
    ).astype(jnp.bfloat16)
    partial_rows = lax.psum_scatter(
        jnp.einsum("pms,pns->mn", coeff, masked, preferred_element_type=jnp.float32),
        "row",
        scatter_dimension=0,
        tiled=True,
    )
    exchange_k = lax.psum_scatter(partial_rows, "col", scatter_dimension=1, tiled=True)
    return exchange_k


def solution(mesh):
    in_specs = (
        P(("row", "col"), None, None),
        P(("row", "col"), None),
        P(("row", "col"), None, None),
        P(),
    )
    out_specs = P("row", "col")
    return jax.shard_map(local, mesh=mesh, in_specs=in_specs, out_specs=out_specs, check_vma=False)
```

profile of v0, /device:TPU:0, one launch (start us, length us, event | category | flops | bytes accessed | tf_op | source)
XLA Modules:
  0.0 221.1 jit_solution(10216607355251909733)
XLA Ops:
  6.5 0.0 all-gather.2.cloned.1.call-start
  6.5 0.7 all-gather.2.cloned.1.call-update
  7.3 0.0 reduce-scatter.5.cloned.1.call-start
  7.3 0.7 convert_element_type.18
  8.0 4.4 %mul.27 = bf16[4,8,128,8,128]{4,3,2,1,0:T(8,128)(2,1)} broadcast(bf16[4,8,8]{2,1,0:T(8,128)(2,1)S(1)} %convert_element_type.18), dimensions={0,1,3} | broadcast | bytes 8389120 | tf_op jit(solution)/shard_map/mul | solution.py:15
  12.4 0.0 copy-start
  12.4 13.3 %mul.28 = bf16[4,1024,1024]{2,1,0:T(8,128)(2,1)} reshape(bf16[4,8,128,8,128]{4,3,2,1,0:T(8,128)(2,1)} %mul.27) | data formatting | bytes 16777216 | tf_op jit(solution)/shard_map/mul | solution.py:15
  25.7 0.0 copy-done
  25.7 0.1 fusion.13
  25.8 52.2 %all-gather.2.cloned.1.call-done = bf16[1024,1024]{1,0:T(8,128)(2,1)} async-done(((bf16[8,1024]{1,0:T(8,128)(2,1)}), bf16[1024,1024]{1,0:T(8,128)(2,1)}) %all-gather.2.cloned.1.call-update) | async-done | bytes 2097168 | tf_op jit(solution)/shard_map/all_gather | solution.py:25
  78.1 26.5 %fusion.4 = f32[1024,1024]{1,0:T(8,128)} fusion(bf16[4,1024,1024]{2,1,0:T(8,128)(2,1)} %param.4, bf16[4,1024,1024]{2,1,0:T(8,128)(2,1)} %mul.28, bf16[1024]{0:T(1024)(128)(2,1)S(1)} %fusion.13, bf16[1024,1024]{1,0:T(8,128)(2,1)} %all-gather.2.cloned.1.call-done), kind=kOutput, calls=%fused_computation.4 | convolution fusion | flops 17209229312 | bytes 23070720 | tf_op jit(solution)/shard_map/pms,pns->mn/dot_general | solution.py:30
  104.6 0.0 reduce-scatter.5.cloned.1.call-update
  104.6 0.0 reduce-scatter.7.cloned.1.call-start
  104.6 35.7 %reduce-scatter.5.cloned.1.call-done = f32[128,1024]{1,0:T(8,128)} async-done(((f32[1024,1024]{1,0:T(8,128)}), f32[128,1024]{1,0:T(8,128)}) %reduce-scatter.5.cloned.1.call-update) | async-done | bytes 524304 | tf_op jit(solution)/shard_map/reduce_scatter | solution.py:29
  140.4 2.0 copy.7
  142.4 0.0 reduce-scatter.7.cloned.1.call-update
  142.4 72.1 %reduce-scatter.7.cloned.1.call-done = f32[64,128]{1,0:T(8,128)} async-done(((f32[1024,128]{1,0:T(8,128)}), f32[64,128]{1,0:T(8,128)}) %reduce-scatter.7.cloned.1.call-update) | async-done | bytes 32784
Async XLA Ops:
  6.5 71.5 %all-gather.2.cloned.1.call-start = ((), (), s32[]{:S(2)}) async-start(), calls=%async_computation.2 | async-start | bytes 2113536 | tf_op jit(solution)/shard_map/all_gather | solution.py:25
  7.3 133.1 %reduce-scatter.5.cloned.1.call-start = ((), (), s32[]{:S(2)}) async-start(), calls=%async_computation.3 | async-start | bytes 4718592 | tf_op jit(solution)/shard_map/reduce_scatter | solution.py:29
  12.4 13.3 %copy-start = (s32[8]{0:T(128)S(1)}, s32[8]{0:T(128)}, u32[]{:S(2)}) copy-start(s32[8]{0:T(128)} %param.7) | copy-start | bytes 100
  104.6 110.0 %reduce-scatter.7.cloned.1.call-start = ((), (), s32[]{:S(2)}) async-start(), calls=%async_computation.4 | async-start | bytes 557056
Sparse Core Ops, SparseCore 0:
  10.3 67.6 all-gather.1
  104.7 35.6 reduce-scatter.4
  143.6 70.9 reduce-scatter.6
where the time goes:
time: 222 us; the launch traced here: 221 us
  waiting for transfers between devices  161 us (73%)
  matrix products  26.5 us (12%)
  local copies, waits for them, and re-layouts  19.8 us (9%)
  between operations  13.1 us (6%)
    unnamed x4, waiting for transfers between devices  72.9 us
    all_gather x1, waiting for transfers between devices, local(): whole_density = lax.all_gather(density, ('row', 'col'), axis=0, tiled=True)  52.2 us
    reduce_scatter x1, waiting for transfers between devices, local(): lax.psum_scatter(jnp.einsum('pms,pns->mn', coeff, masked, preferred_eleme...  35.7 us
    dot_general x1, matrix products, local(): jnp.einsum('pms,pns->mn', coeff, masked, preferred_element_type=jnp.float32)  26.5 us
    mul x2, local copies, waits for them, and re-layouts, mask_aux(): shaped = shaped * pattern[:, :, None, :, None].astype(aux_ints.dtype)  17.7 us
  transfers between devices with their start and end apart: 3, of which 3 were waited for; matrix products, arithmetic and copies ran while one was open for 8% of the time, Pallas kernels for 0%

commit v1 on v0

v1 whole, which is shorter than its diff:
```python
import functools

import jax
import jax.numpy as jnp
from jax import lax
from jax.experimental import pallas as pl
from jax.experimental.pallas import tpu as pltpu
from jax.sharding import Mesh, PartitionSpec as P

F32 = jnp.float32
BF16 = jnp.bfloat16
BS = 128
NB = 8
N = BS * NB
P_DEV = 4
HALF = N // 2
TILE = 256
NN = (((1,), (0,)), ((), ()))
NT = (((1,), (1,)), ((), ()))
CHIPS = ("z", "x", "y")


def column_mask(sizes_ref):
    lane = lax.broadcasted_iota(jnp.int32, (1, BS), 1)
    return jnp.concatenate([(lane < sizes_ref[b]).astype(F32) for b in range(NB)], axis=1)


def partial_kernel(place_ref, sizes_ref, pattern_ref, aux_hbm, mine_ref, theirs_ref, out_ref, dens, aux, coeff, sems):
    core, side = place_ref[0], place_ref[1]
    copies = [pltpu.make_async_copy(aux_hbm.at[p], aux.at[p], sems.at[p]) for p in range(P_DEV)]
    for copy in copies:
        copy.start()

    cols = column_mask(sizes_ref)
    row = lax.broadcasted_iota(jnp.int32, (BS, 1), 0)
    for z in range(NB // 2):
        for half_ref, c in ((mine_ref, core), (theirs_ref, 1 - core)):
            b = 2 * z + c
            keep = (row < sizes_ref[b]).astype(F32) * cols
            start = pl.multiple_of(b * BS, BS)
            dens[pl.ds(start, BS), :] = half_ref[z * BS:(z + 1) * BS, :] * keep.astype(BF16)

    for p in range(P_DEV):
        copies[p].wait()
        near = [pattern_ref[p, b, b] for b in range(NB)]
        count = functools.reduce(lambda a, b: a + b, near)

        @pl.when(count < NB)
        def _():
            ones = jnp.ones((1, BS), F32)
            wide = jnp.concatenate([ones * w.astype(F32) for w in near], axis=1)
            for b in range(NB):
                factor = (wide * near[b].astype(F32)).astype(BF16)
                aux[p, b * BS:(b + 1) * BS, :] = aux[p, b * BS:(b + 1) * BS, :] * factor

        rows = jnp.concatenate(
            [aux[p, pl.ds(pl.multiple_of((2 * z + side) * BS, BS), BS), :] for z in range(NB // 2)], axis=0
        )
        for t in range(N // TILE):
            s = slice(t * TILE, (t + 1) * TILE)
            coeff[p, :, s] = lax.dot_general(rows, dens[:, s], NN, preferred_element_type=F32).astype(BF16)

    for t in range(HALF // TILE):
        s = slice(t * TILE, (t + 1) * TILE)
        total = lax.dot_general(aux[0], coeff[0, s, :], NT, preferred_element_type=F32)
        for p in range(1, P_DEV):
            total += lax.dot_general(aux[p], coeff[p, s, :], NT, preferred_element_type=F32)
        for h in range(TILE // BS):
            out_ref[t * (TILE // BS) + h] = total[:, h * BS:(h + 1) * BS]


def partial_sums(place, sizes, pattern, aux_ints, mine, theirs):
    smem = pl.BlockSpec(memory_space=pltpu.SMEM)
    vmem = pl.BlockSpec(memory_space=pltpu.VMEM)
    return pl.pallas_call(
        partial_kernel,
        in_specs=[smem, smem, smem, pl.BlockSpec(memory_space=pl.ANY), vmem, vmem],
        out_specs=vmem,
        out_shape=jax.ShapeDtypeStruct((NB // 2, N, BS), F32),
        scratch_shapes=[
            pltpu.VMEM((N, N), BF16),
            pltpu.VMEM((P_DEV, N, N), BF16),
            pltpu.VMEM((P_DEV, HALF, N), BF16),
            pltpu.SemaphoreType.DMA((P_DEV,)),
        ],
        compiler_params=pltpu.CompilerParams(vmem_limit_bytes=40 * 2**20),
        cost_estimate=pl.CostEstimate(flops=P_DEV * 2 * N * N * N, bytes_accessed=2 * P_DEV * N * N, transcendentals=0),
    )(place, sizes, pattern, aux_ints, mine, theirs)


def finish_kernel(place_ref, sizes_ref, parts_ref, out_ref):
    total = jnp.sum(parts_ref[...].astype(F32), axis=0)
    mu = lax.broadcasted_iota(jnp.int32, (BS // 2, BS), 1)
    nu = lax.broadcasted_iota(jnp.int32, (BS // 2, BS), 0)
    xy = place_ref[1]
    nu = nu + (xy % 2) * (BS // 2)
    keep = (mu < sizes_ref[place_ref[0]]) & (nu < sizes_ref[xy // 2])
    out_ref[...] = jnp.where(keep, total, 0.0).T


def finish(place, sizes, parts):
    smem = pl.BlockSpec(memory_space=pltpu.SMEM)
    vmem = pl.BlockSpec(memory_space=pltpu.VMEM)
    return pl.pallas_call(
        finish_kernel,
        in_specs=[smem, smem, vmem],
        out_specs=vmem,
        out_shape=jax.ShapeDtypeStruct((BS, BS // 2), F32),
        compiler_params=pltpu.CompilerParams(vmem_limit_bytes=16 * 2**20),
    )(place, sizes, parts)


def local(aux_ints, density, pattern, block_sizes):
    z, c, x, y = (lax.axis_index(a) for a in ("z", "c", "x", "y"))
    swap = [(0, 1), (1, 0)]
    spread = jnp.broadcast_to(density[None], (64, 8, N))
    mine = lax.all_to_all(spread, CHIPS, 0, 0).reshape(HALF, N)
    theirs = lax.ppermute(mine, "c", swap)
    send = partial_sums(jnp.stack([c, 1 - c]), block_sizes, pattern, aux_ints, mine, theirs)
    got = lax.ppermute(send, "c", swap)
    keep = partial_sums(jnp.stack([c, c]), block_sizes, pattern, aux_ints, mine, theirs)
    chip = (keep + got).astype(BF16).reshape(64, BS // 2, BS)
    parts = lax.all_to_all(chip, CHIPS, 0, 0)
    return finish(jnp.stack([2 * z + c, 4 * x + y]), block_sizes, parts)


def solution(mesh):
    whole = Mesh(mesh.devices.reshape(4, 2, 4, 4), ("z", "c", "x", "y"))
    everywhere = ("z", "c", "x", "y")
    in_specs = (P(everywhere, None, None), P(everywhere, None), P(everywhere, None, None), P())
    return jax.shard_map(local, mesh=whole, in_specs=in_specs, out_specs=P(("z", "c"), ("x", "y")), check_vma=False)
```

time: 222 us -> 88.1 us (0.40)
  waiting for transfers between devices: 161 us -> 21.7 us
  blocking collectives: 0 us -> 30 us
  matrix products: 26.5 us -> 0 us
  Pallas kernels: 0 us -> 24 us
  local copies, waits for them, and re-layouts: 19.8 us -> 4.94 us
  between operations: 13.1 us -> 0.06 us
  starting transfers between devices: 0.08 us -> 5.52 us
    unnamed x4 -> x0, waiting for transfers between devices: 72.9 us -> none
    all_gather x1 -> x0, waiting for transfers between devices: 52.2 us -> none  [local(): whole_density = lax.all_gather(density, ('row', 'col'), axis=0, tiled=True)]
    reduce_scatter x1 -> x0, waiting for transfers between devices: 35.7 us -> none  [local(): lax.psum_scatter(jnp.einsum('pms,pns->mn', coeff, masked, preferred_eleme...]
    all_to_all x0 -> x1, blocking collectives: none -> 30 us  [local(): mine = lax.all_to_all(spread, CHIPS, 0, 0).reshape(HALF, N)]
    dot_general x1 -> x0, matrix products: 26.5 us -> none  [local(): jnp.einsum('pms,pns->mn', coeff, masked, preferred_element_type=jnp.float32)]
    pallas_call x0 -> x3, Pallas kernels: none -> 24 us  [the longest x2 23.2 us: partial_sums(): pl.pallas_call(partial_kernel, in_specs=[smem, smem, smem, pl.BlockSpec(m...]
    all_to_all x0 -> x1, waiting for transfers between devices: none -> 19.1 us  [local(): parts = lax.all_to_all(chip, CHIPS, 0, 0)]
    mul x2 -> x0, local copies, waits for them, and re-layouts: 17.7 us -> none  [mask_aux(): shaped = shaped * pattern[:, :, None, :, None].astype(aux_ints.dtype)]
  transfers between devices with their start and end apart: 3 -> 3, of which waited for: 3 -> 2; matrix products, arithmetic and copies ran while one was open for 8% -> 0% of each run, Pallas kernels for 0% -> 13%
where the time goes in v1:
time: 88.1 us; the launch traced here: 87.7 us
  blocking collectives  30 us (34%)
  Pallas kernels  24 us (27%)
  waiting for transfers between devices  21.7 us (25%)
  starting transfers between devices  5.52 us (6%)
  local copies, waits for them, and re-layouts  4.94 us (6%)
  other arithmetic  1.4 us (2%)
    all_to_all x1, blocking collectives, local(): mine = lax.all_to_all(spread, CHIPS, 0, 0).reshape(HALF, N)  30 us
    pallas_call x2, Pallas kernels, partial_sums(): pl.pallas_call(partial_kernel, in_specs=[smem, smem, smem, pl.BlockSpec(m...  23.2 us
    all_to_all x1, waiting for transfers between devices, local(): parts = lax.all_to_all(chip, CHIPS, 0, 0)  19.1 us
    all_to_all x1, starting transfers between devices, local(): parts = lax.all_to_all(chip, CHIPS, 0, 0)  5.01 us
    unnamed x6, local copies, waits for them, and re-layouts  3.39 us
    ppermute x1, waiting for transfers between devices, local(): theirs = lax.ppermute(mine, 'c', swap)  2.58 us
  transfers between devices with their start and end apart: 3, of which 2 were waited for; matrix products, arithmetic and copies ran while one was open for 0% of the time, Pallas kernels for 13%

profile of v1, /device:TPU:0, one launch (start us, length us, event | category | flops | bytes accessed | tf_op | source)
XLA Modules:
  0.0 87.7 jit_solution(15417408819493256124)
XLA Ops:
  0.0 0.0 copy-start
  0.0 0.0 copy-start.2
  0.0 0.9 broadcast_in_dim.2
  0.9 30.0 %all_to_all.10 = bf16[64,8,1024]{2,1,0:T(8,128)(2,1)S(1)} all-to-all(bf16[64,8,1024]{2,1,0:T(8,128)(2,1)S(1)} %broadcast_in_dim.2), channel_id=1, replica_groups=mesh['z'=4,'c'=2,'x'=4,'y'=4] {'z','x','y'}, dimensions={0} | all-to-all | bytes 2097152 | tf_op jit(solution)/shard_map/all_to_all | solution.py:117
  30.9 0.0 collective-permute-start
  30.9 0.1 pad_add_fusion.2.place_ref
  31.0 2.6 %collective-permute-done.theirs_ref = bf16[512,1024]{1,0:T(8,128)(2,1)S(1)} collective-permute-done((bf16[512,1024]{1,0:T(8,128)(2,1)S(1)}, bf16[512,1024]{1,0:T(8,128)(2,1)S(1)}, u32[]{:S(2)}, u32[]{:S(2)}) %collective-permute-start) | collective-permute-done | bytes 1048608 | tf_op jit(solution)/shard_map/ppermute | solution.py:118
  33.5 0.0 copy-done
  33.5 0.0 copy-done.2
  33.5 0.0 copy-start.1
  33.5 3.4 %copy-done.1 = bf16[4,1024,1024]{2,1,0:T(8,128)(2,1)S(1)} copy-done((bf16[4,1024,1024]{2,1,0:T(8,128)(2,1)S(1)}, bf16[4,1024,1024]{2,1,0:T(8,128)(2,1)}, u32[]{:S(2)}) %copy-start.1) | copy-done | bytes 8388632
  36.9 11.5 %shard_map.47 = f32[4,1024,128]{2,1,0:T(8,128)S(1)} custom-call(s32[2]{0:T(128)S(1)} %pad_add_fusion.2.place_ref, s32[8]{0:T(128)S(1)} %copy-done, s32[4,8,8]{2,1,0:T(8,128)S(1)} %copy-done.2, bf16[4,1024,1024]{2,1,0:T(8,128)(2,1)S(1)} %copy-done.1, bf16[512,1024]{1,0:T(8,128)(2,1)S(1)} %bitcast.7, bf16[512,1024]{1,0:T(8,128)(2,1)S(1)} %collective-permute-done.theirs_ref), custom_call_target="tpu_custom_call" | custom-call | flops 8589934592 | bytes 8388608 | tf_op jit(solution)/shard_map/pallas_call | solution.py:75
  48.4 0.5 collective-permute-start.1
  49.0 0.1 pad_add_fusion.1.place_ref
  49.0 11.7 %shard_map.46 = f32[4,1024,128]{2,1,0:T(8,128)S(1)} custom-call(s32[2]{0:T(128)S(1)} %pad_add_fusion.1.place_ref, s32[8]{0:T(128)S(1)} %copy-done, s32[4,8,8]{2,1,0:T(8,128)S(1)} %copy-done.2, bf16[4,1024,1024]{2,1,0:T(8,128)(2,1)S(1)} %copy-done.1, bf16[512,1024]{1,0:T(8,128)(2,1)S(1)} %bitcast.8, bf16[512,1024]{1,0:T(8,128)(2,1)S(1)} %collective-permute-done.theirs_ref), custom_call_target="tpu_custom_call" | custom-call | flops 8589934592 | bytes 8388608 | tf_op jit(solution)/shard_map/pallas_call | solution.py:75
  60.7 0.0 collective-permute-done.1
  60.7 1.2 %add_convert_fusion = bf16[4,1024,128]{2,1,0:T(8,128)(2,1)} fusion(f32[4,1024,128]{2,1,0:T(8,128)S(1)} %shard_map.46, f32[4,1024,128]{2,1,0:T(8,128)S(1)} %collective-permute-done.1), kind=kLoop, calls=%fused_computation | loop fusion | flops 1048576 | bytes 5242880 | tf_op jit(solution)/shard_map/convert_element_type | solution.py:122
  61.9 5.0 %all-to-all-start.1 = ((bf16[64,64,128]{2,1,0:T(8,128)(2,1)}), bf16[64,64,128]{2,1,0:T(8,128)(2,1)S(1)}, u32[]{:S(2)}, u32[]{:S(2)}) async-start(bf16[64,64,128]{2,1,0:T(8,128)(2,1)} %bitcast.5), calls=%async_computation.1 | async-start | bytes 2097152 | tf_op jit(solution)/shard_map/all_to_all | solution.py:123
  66.9 0.1 pad_add_fusion.place_ref
  67.0 19.1 %all-to-all-done.1.parts_ref = bf16[64,64,128]{2,1,0:T(8,128)(2,1)S(1)} async-done(((bf16[64,64,128]{2,1,0:T(8,128)(2,1)}), bf16[64,64,128]{2,1,0:T(8,128)(2,1)S(1)}, u32[]{:S(2)}, u32[]{:S(2)}) %all-to-all-start.1) | async-done | bytes 1048608 | tf_op jit(solution)/shard_map/all_to_all | solution.py:123
  86.2 0.8 shard_map.48
  87.0 0.7 copy.5
Async XLA Ops:
  0.0 33.5 %copy-start = (s32[8]{0:T(128)S(1)}, s32[8]{0:T(128)}, u32[]{:S(2)}) copy-start(s32[8]{0:T(128)} %sizes_ref.5) | copy-start | bytes 100
  0.0 33.5 %copy-start.2 = (s32[4,8,8]{2,1,0:T(8,128)S(1)}, s32[4,8,8]{2,1,0:T(8,128)}, u32[]{:S(2)}) copy-start(s32[4,8,8]{2,1,0:T(8,128)} %pattern_ref.3) | copy-start | bytes 3076
  30.9 2.7 %collective-permute-start = (bf16[512,1024]{1,0:T(8,128)(2,1)S(1)}, bf16[512,1024]{1,0:T(8,128)(2,1)S(1)}, u32[]{:S(2)}, u32[]{:S(2)}) collective-permute-start(bf16[512,1024]{1,0:T(8,128)(2,1)S(1)} %bitcast.6), channel_id=1, source_target_pairs={{0,16},{16,0},{1,17},{17,1},{2,18},{18,2},{3,19},{19,3},{4,20},{20... | collective-permute-start | bytes 3145736 | tf_op jit(solution)/shard_map/ppermute | solution.py:118
  33.5 3.4 %copy-start.1 = (bf16[4,1024,1024]{2,1,0:T(8,128)(2,1)S(1)}, bf16[4,1024,1024]{2,1,0:T(8,128)(2,1)}, u32[]{:S(2)}) copy-start(bf16[4,1024,1024]{2,1,0:T(8,128)(2,1)} %aux_hbm.3) | copy-start | bytes 25165828
  48.4 12.3 %collective-permute-start.1 = (f32[4,1024,128]{2,1,0:T(8,128)S(1)}, f32[4,1024,128]{2,1,0:T(8,128)S(1)}, u32[]{:S(2)}, u32[]{:S(2)}) collective-permute-start(f32[4,1024,128]{2,1,0:T(8,128)S(1)} %shard_map.47), channel_id=1, source_target_pairs={{0,16},{16,0},{1,17},{17,1},{2,18},{18,2},{3,19},{19,3},{4,20},{20... | collective-permute-start | bytes 6291464 | tf_op jit(solution)/shard_map/ppermute | solution.py:120
  61.9 24.2 %all-to-all-start.1 = ((bf16[64,64,128]{2,1,0:T(8,128)(2,1)}), bf16[64,64,128]{2,1,0:T(8,128)(2,1)S(1)}, u32[]{:S(2)}, u32[]{:S(2)}) async-start(bf16[64,64,128]{2,1,0:T(8,128)(2,1)} %bitcast.5), calls=%async_computation.1 | async-start | bytes 2097152 | tf_op jit(solution)/shard_map/all_to_all | solution.py:123

commit v2 on v0

v2 whole, which is shorter than its diff:
```python
import jax
import jax.numpy as jnp
from jax import lax
from jax.experimental import pallas as pl
from jax.experimental.pallas import tpu as pltpu
from jax.sharding import Mesh, PartitionSpec as P

F32 = jnp.float32
BF16 = jnp.bfloat16
BS = 128
NB = 8
N = BS * NB
P_DEV = 4
WIDE = P_DEV * N
HALF = N // 2
TILE = 256
PIECES = 4
AHEAD = 4
CHIP_COUNT = 64
ROWS = 8
NN = (((1,), (0,)), ((), ()))
NT = (((1,), (1,)), ((), ()))
CHIPS = ("z", "x", "y")
SMEM = pl.BlockSpec(memory_space=pltpu.SMEM)
HBM = pl.BlockSpec(memory_space=pltpu.HBM)
VMEM = pl.BlockSpec(memory_space=pltpu.VMEM)


def params(mib):
    return pltpu.CompilerParams(vmem_limit_bytes=mib * 2**20)


def prepare_kernel(sizes, pattern, aux, out):
    p = pl.program_id(0)
    lane = lax.broadcasted_iota(jnp.int32, (1, BS), 1)
    row = lax.broadcasted_iota(jnp.int32, (BS, 1), 0)
    near = [pattern[p, b, b] for b in range(NB)]
    cols = jnp.concatenate([((lane < sizes[b]) & (near[b] > 0)).astype(F32) for b in range(NB)], axis=1)
    for b in range(NB):
        rows = ((row < sizes[b]) & (near[b] > 0)).astype(F32)
        at = slice(b * BS, (b + 1) * BS)
        out[at, :] = aux[0, at, :] * (rows * cols).astype(BF16)


def prepare(sizes, pattern, aux):
    return pl.pallas_call(
        prepare_kernel,
        grid=(P_DEV,),
        in_specs=[SMEM, SMEM, pl.BlockSpec((1, N, N), lambda p: (p, 0, 0))],
        out_specs=pl.BlockSpec((N, N), lambda p: (0, p)),
        out_shape=pltpu.HBM((N, WIDE), BF16),
        compiler_params=params(48),
        cost_estimate=pl.CostEstimate(flops=0, bytes_accessed=2 * 2 * N * WIDE, transcendentals=0),
    )(sizes, pattern, aux)


def block(index):
    return pl.ds(pl.multiple_of(index * BS, BS), BS)


def gather_rows(p, side, order, aux):
    return jnp.concatenate(
        [
            jnp.concatenate([aux[block(2 * z + side), block(p * NB + k)] for k in order], axis=1)
            for z in range(NB // 2)
        ],
        axis=0,
    )


def blocks_of(core):
    return [2 * z + core for z in range(NB // 2)]


def tiles(p):
    for t in range(N // TILE):
        yield slice(t * TILE, (t + 1) * TILE), slice(p * N + t * TILE, p * N + (t + 1) * TILE)


def half_sums(aux, coeff, store):
    for t in range(HALF // TILE):
        value = lax.dot_general(aux[...], coeff[t * TILE:(t + 1) * TILE, :], NT, preferred_element_type=F32)
        for h in range(TILE // BS):
            store(t * (TILE // BS) + h, value[:, h * BS:(h + 1) * BS])


def first_kernel(place, aux_hbm, mine, part, aux, sems):
    depth = N // PIECES

    def copies(p):
        pieces = []
        for i in range(PIECES):
            at = (slice(i * depth, (i + 1) * depth), slice(p * N, (p + 1) * N))
            pieces.append(pltpu.make_async_copy(aux_hbm.at[at], aux.at[at], sems.at[p, i]))
        return pieces

    for p in range(AHEAD):
        for copy in copies(p):
            copy.start()
    for p in range(P_DEV):
        for copy in copies(p):
            copy.wait()
        if p + AHEAD < P_DEV:
            for copy in copies(p + AHEAD):
                copy.start()
        rows = gather_rows(p, 1 - place[1], blocks_of(place[1]), aux)
        for s, at in tiles(p):
            part[:, at] = lax.dot_general(rows, mine[:, s], NN, preferred_element_type=F32)


def first_part(place, aux, mine):
    return pl.pallas_call(
        first_kernel,
        in_specs=[SMEM, HBM, VMEM],
        out_specs=[VMEM, VMEM],
        out_shape=[jax.ShapeDtypeStruct((HALF, WIDE), F32), jax.ShapeDtypeStruct((N, WIDE), BF16)],
        scratch_shapes=[pltpu.SemaphoreType.DMA((P_DEV, PIECES))],
        compiler_params=params(30),
        cost_estimate=pl.CostEstimate(flops=N * N * WIDE // 2, bytes_accessed=0, transcendentals=0),
    )(place, aux, mine)


def send_kernel(place, aux, theirs, part, out, coeff):
    for p in range(P_DEV):
        rows = gather_rows(p, 1 - place[1], blocks_of(1 - place[1]), aux)
        for s, at in tiles(p):
            value = lax.dot_general(rows, theirs[:, s], NN, preferred_element_type=F32)
            coeff[:, at] = (part[:, at] + value).astype(BF16)

    def store(z, value):
        out[z] = value

    half_sums(aux, coeff, store)


def send_sums(place, aux, theirs, part):
    return pl.pallas_call(
        send_kernel,
        in_specs=[SMEM, VMEM, VMEM, VMEM],
        out_specs=VMEM,
        out_shape=jax.ShapeDtypeStruct((NB // 2, N, BS), F32),
        scratch_shapes=[pltpu.VMEM((HALF, WIDE), BF16)],
        compiler_params=params(20),
        cost_estimate=pl.CostEstimate(flops=3 * N * N * WIDE // 2, bytes_accessed=0, transcendentals=0),
    )(place, aux, theirs, part)


def keep_coeff_kernel(place, aux, mine, theirs, coeff):
    order = blocks_of(place[1]) + blocks_of(1 - place[1])
    for p in range(P_DEV):
        rows = gather_rows(p, place[1], order, aux)
        for s, at in tiles(p):
            dens = jnp.concatenate([mine[:, s], theirs[:, s]], axis=0)
            coeff[:, at] = lax.dot_general(rows, dens, NN, preferred_element_type=F32).astype(BF16)


def keep_coeff(place, aux, mine, theirs):
    return pl.pallas_call(
        keep_coeff_kernel,
        in_specs=[SMEM, VMEM, VMEM, VMEM],
        out_specs=VMEM,
        out_shape=jax.ShapeDtypeStruct((HALF, WIDE), BF16),
        compiler_params=params(20),
        cost_estimate=pl.CostEstimate(flops=N * N * WIDE, bytes_accessed=0, transcendentals=0),
    )(place, aux, mine, theirs)


def keep_sums_kernel(aux, coeff, got, out):
    def store(z, value):
        out[z] = (value + got[z]).astype(BF16)

    half_sums(aux, coeff, store)


def keep_sums(aux, coeff, got):
    return pl.pallas_call(
        keep_sums_kernel,
        in_specs=[VMEM, VMEM, VMEM],
        out_specs=VMEM,
        out_shape=jax.ShapeDtypeStruct((NB // 2, N, BS), BF16),
        compiler_params=params(20),
        cost_estimate=pl.CostEstimate(flops=N * N * WIDE, bytes_accessed=0, transcendentals=0),
    )(aux, coeff, got)


def finish_kernel(parts, out):
    out[...] = jnp.sum(parts[...].astype(F32), axis=0)


def finish(parts):
    return pl.pallas_call(
        finish_kernel,
        in_specs=[VMEM],
        out_specs=VMEM,
        out_shape=jax.ShapeDtypeStruct((BS // 2, BS), F32),
        compiler_params=params(16),
    )(parts)


def local(aux_ints, density, pattern, block_sizes):
    place = jnp.stack([lax.axis_index("z"), lax.axis_index("c")])
    swap = [(0, 1), (1, 0)]
    everyone = jnp.broadcast_to(density[None], (CHIP_COUNT, ROWS, N))
    mine = lax.all_to_all(everyone, CHIPS, 0, 0).reshape(HALF, N)
    mine, masked = lax.optimization_barrier((mine, prepare(block_sizes, pattern, aux_ints)))
    theirs = lax.ppermute(mine, "c", swap)
    part, aux = first_part(place, masked, mine)
    got = lax.ppermute(send_sums(place, aux, theirs, part), "c", swap)
    chip = keep_sums(aux, keep_coeff(place, aux, mine, theirs), got)
    parts = lax.all_to_all(chip.reshape(CHIP_COUNT, BS // 2, BS), CHIPS, 0, 0)
    return finish(parts).T


def solution(mesh):
    whole = Mesh(mesh.devices.reshape(4, 2, 4, 4), ("z", "c", "x", "y"))
    everywhere = ("z", "c", "x", "y")
    in_specs = (P(everywhere, None, None), P(everywhere, None), P(everywhere, None, None), P())
    return jax.shard_map(local, mesh=whole, in_specs=in_specs, out_specs=P(("z", "c"), ("x", "y")), check_vma=False)
```

time: 222 us -> 79.8 us (0.36)
  waiting for transfers between devices: 161 us -> 9.82 us
  Pallas kernels: 0 us -> 30.4 us
  matrix products: 26.5 us -> 0 us
  blocking collectives: 0 us -> 23.5 us
  local copies, waits for them, and re-layouts: 19.8 us -> 3.26 us
  between operations: 13.1 us -> 0.07 us
  starting transfers between devices: 0.08 us -> 12.3 us
    unnamed x4 -> x0, waiting for transfers between devices: 72.9 us -> none
    all_gather x1 -> x0, waiting for transfers between devices: 52.2 us -> none  [local(): whole_density = lax.all_gather(density, ('row', 'col'), axis=0, tiled=True)]
    reduce_scatter x1 -> x0, waiting for transfers between devices: 35.7 us -> none  [local(): lax.psum_scatter(jnp.einsum('pms,pns->mn', coeff, masked, preferred_eleme...]
    pallas_call x0 -> x6, Pallas kernels: none -> 30.4 us  [the longest x1 7.52 us: prepare(): pl.pallas_call(prepare_kernel, grid=(P_DEV,), in_specs=[SMEM, SMEM, pl.Bl...]
    dot_general x1 -> x0, matrix products: 26.5 us -> none  [local(): jnp.einsum('pms,pns->mn', coeff, masked, preferred_element_type=jnp.float32)]
    all_to_all x0 -> x1, blocking collectives: none -> 23.5 us  [local(): parts = lax.all_to_all(chip.reshape(CHIP_COUNT, BS // 2, BS), CHIPS, 0, 0)]
    mul x2 -> x0, local copies, waits for them, and re-layouts: 17.7 us -> none  [mask_aux(): shaped = shaped * pattern[:, :, None, :, None].astype(aux_ints.dtype)]
    all_to_all x0 -> x1, starting transfers between devices: none -> 11.5 us  [local(): mine = lax.all_to_all(everyone, CHIPS, 0, 0).reshape(HALF, N)]
  transfers between devices with their start and end apart: 3 -> 3, of which waited for: 3 -> 1; matrix products, arithmetic and copies ran while one was open for 8% -> 0% of each run, Pallas kernels for 0% -> 22%
where the time goes in v2:
time: 79.8 us; the launch traced here: 79.4 us
  Pallas kernels  30.4 us (38%)
  blocking collectives  23.5 us (29%)
  starting transfers between devices  12.3 us (15%)
  waiting for transfers between devices  9.82 us (12%)
  local copies, waits for them, and re-layouts  3.26 us (4%)
    all_to_all x1, blocking collectives, local(): parts = lax.all_to_all(chip.reshape(CHIP_COUNT, BS // 2, BS), CHIPS, 0, 0)  23.5 us
    all_to_all x1, starting transfers between devices, local(): mine = lax.all_to_all(everyone, CHIPS, 0, 0).reshape(HALF, N)  11.5 us
    all_to_all x1, waiting for transfers between devices, local(): mine = lax.all_to_all(everyone, CHIPS, 0, 0).reshape(HALF, N)  9.82 us
    pallas_call x1, Pallas kernels, prepare(): pl.pallas_call(prepare_kernel, grid=(P_DEV,), in_specs=[SMEM, SMEM, pl.Bl...  7.52 us
    pallas_call x1, Pallas kernels, send_sums(): pl.pallas_call(send_kernel, in_specs=[SMEM, VMEM, VMEM, VMEM], out_specs=...  7.32 us
    pallas_call x1, Pallas kernels, first_part(): pl.pallas_call(first_kernel, in_specs=[SMEM, HBM, VMEM], out_specs=[VMEM,...  5.13 us
    pallas_call x1, Pallas kernels, keep_coeff(): pl.pallas_call(keep_coeff_kernel, in_specs=[SMEM, VMEM, VMEM, VMEM], out_...  5.08 us
    pallas_call x1, Pallas kernels, keep_sums(): pl.pallas_call(keep_sums_kernel, in_specs=[VMEM, VMEM, VMEM], out_specs=V...  4.52 us
  transfers between devices with their start and end apart: 3, of which 1 were waited for; matrix products, arithmetic and copies ran while one was open for 0% of the time, Pallas kernels for 22%

profile of v2, /device:TPU:0, one launch (start us, length us, event | category | flops | bytes accessed | tf_op | source)
XLA Modules:
  0.0 79.4 jit_solution(251595782768668941)
XLA Ops:
  0.0 1.9 %broadcast_in_dim.2 = bf16[64,8,1024]{2,1,0:T(8,128)(2,1)} broadcast(bf16[8,1024]{1,0:T(8,128)(2,1)} %param.5), dimensions={1,2} | broadcast | bytes 1064960 | tf_op jit(solution)/shard_map/broadcast_in_dim | solution.py:203
  1.9 11.5 %all-to-all-start = ((bf16[64,8,1024]{2,1,0:T(8,128)(2,1)}), bf16[64,8,1024]{2,1,0:T(8,128)(2,1)S(1)}, u32[]{:S(2)}, u32[]{:S(2)}) async-start(bf16[64,8,1024]{2,1,0:T(8,128)(2,1)} %broadcast_in_dim.2), calls=%async_computation | async-start | bytes 2097152 | tf_op jit(solution)/shard_map/all_to_all | solution.py:204
  13.4 0.0 copy-start
  13.4 0.7 copy-done
  14.1 0.0 copy-start.1
  14.1 0.7 copy-done.1
  14.8 7.5 %shard_map.46.aux_hbm = bf16[1024,4096]{1,0:T(8,128)(2,1)} custom-call(s32[8]{0:T(128)S(1)} %copy-done.1, s32[4,8,8]{2,1,0:T(8,128)S(1)} %copy-done, bf16[4,1024,1024]{2,1,0:T(8,128)(2,1)} %aux.1), custom_call_target="tpu_custom_call" | custom-call | bytes 16777216 | tf_op jit(solution)/shard_map/pallas_call | solution.py:46
  22.3 9.8 %all-to-all-done = bf16[64,8,1024]{2,1,0:T(8,128)(2,1)S(1)} async-done(((bf16[64,8,1024]{2,1,0:T(8,128)(2,1)}), bf16[64,8,1024]{2,1,0:T(8,128)(2,1)S(1)}, u32[]{:S(2)}, u32[]{:S(2)}) %all-to-all-start) | async-done | bytes 1048608 | tf_op jit(solution)/shard_map/all_to_all | solution.py:204
  32.1 0.0 collective-permute-start
  32.1 0.1 pad_add_fusion.place
  32.2 5.1 %shard_map.47 = (f32[512,4096]{1,0:T(8,128)S(1)}, bf16[1024,4096]{1,0:T(8,128)(2,1)S(1)}) custom-call(s32[2]{0:T(128)S(1)} %pad_add_fusion.place, bf16[1024,4096]{1,0:T(8,128)(2,1)} %shard_map.46.aux_hbm, bf16[512,1024]{1,0:T(8,128)(2,1)S(1)} %bitcast.6), custom_call_target="tpu_custom_call" | custom-call | flops 2147483648 | tf_op jit(solution)/shard_map/pallas_call | solution.py:112
  37.3 0.0 collective-permute-done.theirs
  37.3 7.3 %shard_map.49 = f32[4,1024,128]{2,1,0:T(8,128)S(1)} custom-call(s32[2]{0:T(128)S(1)} %pad_add_fusion.place, bf16[1024,4096]{1,0:T(8,128)(2,1)S(1)} %get-tuple-element.11.aux, bf16[512,1024]{1,0:T(8,128)(2,1)S(1)} %collective-permute-done.theirs, f32[512,4096]{1,0:T(8,128)S(1)} %get-tuple-element.12.part), custom_call_target="tpu_custom_call" | custom-call | flops 6442450944 | tf_op jit(solution)/shard_map/pallas_call | solution.py:137
  44.7 0.8 collective-permute-start.1
  45.4 5.1 %shard_map.48.coeff = bf16[512,4096]{1,0:T(8,128)(2,1)S(1)} custom-call(s32[2]{0:T(128)S(1)} %pad_add_fusion.place, bf16[1024,4096]{1,0:T(8,128)(2,1)S(1)} %get-tuple-element.11.aux, bf16[512,1024]{1,0:T(8,128)(2,1)S(1)} %bitcast.7, bf16[512,1024]{1,0:T(8,128)(2,1)S(1)} %collective-permute-done.theirs), custom_call_target="tpu_custom_call" | custom-call | flops 4294967296 | tf_op jit(solution)/shard_map/pallas_call | solution.py:158
  50.5 0.0 collective-permute-done.1.got
  50.5 4.5 %shard_map.50 = bf16[4,1024,128]{2,1,0:T(8,128)(2,1)S(1)} custom-call(bf16[1024,4096]{1,0:T(8,128)(2,1)S(1)} %get-tuple-element.11.aux, bf16[512,4096]{1,0:T(8,128)(2,1)S(1)} %shard_map.48.coeff, f32[4,1024,128]{2,1,0:T(8,128)S(1)} %collective-permute-done.1.got), custom_call_target="tpu_custom_call" | custom-call | flops 4294967296 | tf_op jit(solution)/shard_map/pallas_call | solution.py:176
  55.1 23.5 %all_to_all.10.parts = bf16[64,64,128]{2,1,0:T(8,128)(2,1)S(1)} all-to-all(bf16[64,64,128]{2,1,0:T(8,128)(2,1)S(1)} %bitcast.8), channel_id=1, replica_groups=mesh['z'=4,'c'=2,'x'=4,'y'=4] {'z','x','y'}, dimensions={0} | all-to-all | bytes 2097152 | tf_op jit(solution)/shard_map/all_to_all | solution.py:210
  78.6 0.8 %shard_map.51 = f32[64,128]{1,0:T(8,128)} custom-call(bf16[64,64,128]{2,1,0:T(8,128)(2,1)S(1)} %all_to_all.10.parts), custom_call_target="tpu_custom_call" | custom-call | tf_op jit(solution)/shard_map/pallas_call | solution.py:191
Async XLA Ops:
  1.9 30.2 %all-to-all-start = ((bf16[64,8,1024]{2,1,0:T(8,128)(2,1)}), bf16[64,8,1024]{2,1,0:T(8,128)(2,1)S(1)}, u32[]{:S(2)}, u32[]{:S(2)}) async-start(bf16[64,8,1024]{2,1,0:T(8,128)(2,1)} %broadcast_in_dim.2), calls=%async_computation | async-start | bytes 2097152 | tf_op jit(solution)/shard_map/all_to_all | solution.py:204
  13.4 0.7 copy-start
  14.1 0.7 copy-start.1
  32.1 5.2 %collective-permute-start = (bf16[512,1024]{1,0:T(8,128)(2,1)S(1)}, bf16[512,1024]{1,0:T(8,128)(2,1)S(1)}, u32[]{:S(2)}, u32[]{:S(2)}) collective-permute-start(bf16[512,1024]{1,0:T(8,128)(2,1)S(1)} %bitcast.5), channel_id=1, source_target_pairs={{0,16},{16,0},{1,17},{17,1},{2,18},{18,2},{3,19},{19,3},{4,20},{20... | collective-permute-start | bytes 3145736 | tf_op jit(solution)/shard_map/ppermute | solution.py:206
  44.7 5.9 %collective-permute-start.1 = (f32[4,1024,128]{2,1,0:T(8,128)S(1)}, f32[4,1024,128]{2,1,0:T(8,128)S(1)}, u32[]{:S(2)}, u32[]{:S(2)}) collective-permute-start(f32[4,1024,128]{2,1,0:T(8,128)S(1)} %shard_map.49), channel_id=1, source_target_pairs={{0,16},{16,0},{1,17},{17,1},{2,18},{18,2},{3,19},{19,3},{4,20},{20... | collective-permute-start | bytes 6291464 | tf_op jit(solution)/shard_map/ppermute | solution.py:208

commit v3 on v2

v3 whole, which is shorter than its diff:
```python
import jax
import jax.numpy as jnp
from jax import lax
from jax.experimental import pallas as pl
from jax.experimental.pallas import tpu as pltpu
from jax.sharding import Mesh, PartitionSpec as P

F32 = jnp.float32
BF16 = jnp.bfloat16
BS = 128
NB = 8
N = BS * NB
P_DEV = 4
WIDE = P_DEV * N
HALF = N // 2
TILE = 256
CHIP_COUNT = 64
ROWS = 8
NN = (((1,), (0,)), ((), ()))
NT = (((1,), (1,)), ((), ()))
CHIPS = ("z", "x", "y")
SMEM = pl.BlockSpec(memory_space=pltpu.SMEM)
VMEM = pl.BlockSpec(memory_space=pltpu.VMEM)


def params(mib):
    return pltpu.CompilerParams(vmem_limit_bytes=mib * 2**20)


def cost(products):
    return pl.CostEstimate(flops=int(products * N * N * WIDE), bytes_accessed=0, transcendentals=0)


def core_order(core):
    return [2 * z + core for z in range(NB // 2)] + [2 * z + 1 - core for z in range(NB // 2)]


def block(index):
    return pl.ds(pl.multiple_of(index * BS, BS), BS)


def prepare_kernel(place, sizes, pattern, aux, send_own, send_other, keep_own, keep_other):
    p = pl.program_id(0)
    lane = lax.broadcasted_iota(jnp.int32, (1, BS), 1)
    row = lax.broadcasted_iota(jnp.int32, (BS, 1), 0)
    order = core_order(place[0])
    cols = [((lane < sizes[b]) & (pattern[p, b, b] > 0)).astype(F32) for b in order]
    outs = ((keep_own, keep_other), (send_own, send_other))
    for i, b in enumerate(order):
        rows = ((row < sizes[b]) & (pattern[p, b, b] > 0)).astype(F32)
        half, at = divmod(i, NB // 2)
        for j, k in enumerate(order):
            value = aux[0, block(b), block(k)] * (rows * cols[j]).astype(BF16)
            other, to = divmod(j, NB // 2)
            outs[half][other][at * BS:(at + 1) * BS, to * BS:(to + 1) * BS] = value


def prepare(place, sizes, pattern, aux):
    quarter = pl.BlockSpec((HALF, HALF), lambda p: (0, p))
    return pl.pallas_call(
        prepare_kernel,
        grid=(P_DEV,),
        in_specs=[SMEM, SMEM, SMEM, pl.BlockSpec((1, N, N), lambda p: (p, 0, 0))],
        out_specs=[quarter] * 4,
        out_shape=[pltpu.HBM((HALF, WIDE // 2), BF16)] * 4,
        compiler_params=params(48),
        cost_estimate=pl.CostEstimate(flops=0, bytes_accessed=2 * 2 * N * WIDE, transcendentals=0),
    )(place, sizes, pattern, aux)


def tiles(p):
    for t in range(N // TILE):
        other, within = divmod(t * TILE, HALF)
        swapped = (1 - other) * HALF + within
        at = other * (WIDE // 2) + p * HALF + within
        yield slice(t * TILE, (t + 1) * TILE), slice(swapped, swapped + TILE), slice(at, at + TILE)


def slab(p):
    return slice(p * HALF, (p + 1) * HALF)


def first_kernel(send_own, mine, part):
    for p in range(P_DEV):
        for s, _, at in tiles(p):
            part[:, at] = lax.dot_general(send_own[:, slab(p)], mine[:, s], NN, preferred_element_type=F32)


def first_part(send_own, mine):
    return pl.pallas_call(
        first_kernel,
        in_specs=[VMEM, VMEM],
        out_specs=VMEM,
        out_shape=jax.ShapeDtypeStruct((HALF, WIDE), F32),
        compiler_params=params(20),
        cost_estimate=cost(0.5),
    )(send_own, mine)


def half_sums(aux, coeff, store):
    send_own, send_other, keep_own, keep_other = aux
    rows = jnp.concatenate(
        [
            jnp.concatenate([send_own[...], send_other[...]], axis=1),
            jnp.concatenate([keep_own[...], keep_other[...]], axis=1),
        ],
        axis=0,
    )
    for t in range(HALF // TILE):
        value = lax.dot_general(rows, coeff[t * TILE:(t + 1) * TILE, :], NT, preferred_element_type=F32)
        for h in range(TILE // BS):
            store(t * (TILE // BS) + h, value[:, h * BS:(h + 1) * BS])


def send_kernel(send_own, send_other, keep_own, keep_other, theirs, part, out, coeff):
    for p in range(P_DEV):
        for s, swapped, at in tiles(p):
            value = lax.dot_general(send_other[:, slab(p)], theirs[:, swapped], NN, preferred_element_type=F32)
            coeff[:, at] = (part[:, at] + value).astype(BF16)

    def store(z, value):
        out[z] = value

    half_sums((send_own, send_other, keep_own, keep_other), coeff, store)


def send_sums(aux, theirs, part):
    return pl.pallas_call(
        send_kernel,
        in_specs=[VMEM] * 6,
        out_specs=VMEM,
        out_shape=jax.ShapeDtypeStruct((NB // 2, N, BS), F32),
        scratch_shapes=[pltpu.VMEM((HALF, WIDE), BF16)],
        compiler_params=params(20),
        cost_estimate=cost(1.5),
    )(*aux, theirs, part)


def keep_coeff_kernel(keep_own, keep_other, mine, theirs, coeff):
    for p in range(P_DEV):
        rows = jnp.concatenate([keep_own[:, slab(p)], keep_other[:, slab(p)]], axis=1)
        for s, swapped, at in tiles(p):
            dens = jnp.concatenate([mine[:, s], theirs[:, swapped]], axis=0)
            coeff[:, at] = lax.dot_general(rows, dens, NN, preferred_element_type=F32).astype(BF16)


def keep_coeff(aux, mine, theirs):
    return pl.pallas_call(
        keep_coeff_kernel,
        in_specs=[VMEM] * 4,
        out_specs=VMEM,
        out_shape=jax.ShapeDtypeStruct((HALF, WIDE), BF16),
        compiler_params=params(20),
        cost_estimate=cost(1),
    )(aux[2], aux[3], mine, theirs)


def keep_sums_kernel(send_own, send_other, keep_own, keep_other, coeff, got, out):
    def store(z, value):
        out[z] = (value + jnp.concatenate([got[z, HALF:, :], got[z, :HALF, :]], axis=0)).astype(BF16)

    half_sums((send_own, send_other, keep_own, keep_other), coeff, store)


def keep_sums(aux, coeff, got):
    return pl.pallas_call(
        keep_sums_kernel,
        in_specs=[VMEM] * 6,
        out_specs=VMEM,
        out_shape=jax.ShapeDtypeStruct((NB // 2, N, BS), BF16),
        compiler_params=params(20),
        cost_estimate=cost(1),
    )(*aux, coeff, got)


def finish_kernel(parts, out):
    out[...] = jnp.sum(parts[...].astype(F32), axis=0)


def finish(parts):
    return pl.pallas_call(
        finish_kernel,
        in_specs=[VMEM],
        out_specs=VMEM,
        out_shape=jax.ShapeDtypeStruct((BS // 2, BS), F32),
        compiler_params=params(16),
    )(parts)


def sums_groups():
    return [
        [(z * 2 + core) * 16 + 2 * b + h for z in range(NB // 2) for b in core_order(1 - core) for h in range(2)]
        for core in range(2)
    ]


def local(aux_ints, density, pattern, block_sizes):
    core = lax.axis_index("c")
    swap = [(0, 1), (1, 0)]
    blocks = density.reshape(ROWS, NB // 2, 2, BS).swapaxes(1, 2)
    blocks = jnp.where(core == 0, blocks, blocks[:, ::-1]).reshape(ROWS, N)
    everyone = jnp.broadcast_to(blocks[None], (CHIP_COUNT, ROWS, N))
    mine = lax.all_to_all(everyone, CHIPS, 0, 0).reshape(HALF, N)
    mine, aux = lax.optimization_barrier((mine, prepare(core[None], block_sizes, pattern, aux_ints)))
    theirs = lax.ppermute(mine, "c", swap)
    part = first_part(aux[0], mine)
    got = lax.ppermute(send_sums(aux, theirs, part), "c", swap)
    chip = keep_sums(aux, keep_coeff(aux, mine, theirs), got)
    chip = chip.reshape(CHIP_COUNT, BS // 2, BS)
    parts = lax.all_to_all(chip, ("z", "c", "x", "y"), 0, 0, axis_index_groups=sums_groups())
    return finish(parts).T


def solution(mesh):
    whole = Mesh(mesh.devices.reshape(4, 2, 4, 4), ("z", "c", "x", "y"))
    everywhere = ("z", "c", "x", "y")
    in_specs = (P(everywhere, None, None), P(everywhere, None), P(everywhere, None, None), P())
    return jax.shard_map(local, mesh=whole, in_specs=in_specs, out_specs=P(("z", "c"), ("x", "y")), check_vma=False)
```

time: 79.8 us -> 78.2 us (0.980)
  Pallas kernels: 30.4 us -> 26.6 us
  waiting for transfers between devices: 9.82 us -> 11 us
    pallas_call x5, Pallas kernels: 29.6 us -> 25.8 us  [the longest x1 7.73 us: prepare(): pl.pallas_call(prepare_kernel, grid=(P_DEV,), in_specs=[SMEM, SMEM, SMEM,...]
    all_to_all x1, waiting for transfers between devices: 9.82 us -> 11 us  [local(): mine = lax.all_to_all(everyone, CHIPS, 0, 0).reshape(HALF, N)]
    select_n x0 -> x1, other arithmetic: none -> 0.8 us  [local(): blocks = jnp.where(core == 0, blocks, blocks[:, ::-1]).reshape(ROWS, N)]
    unnamed x4 -> x14, local copies, waits for them, and re-layouts: 1.37 us -> 2.09 us
  transfers between devices with their start and end apart: 3 -> 3, of which waited for: 1 -> 1; matrix products, arithmetic and copies ran while one was open for 0% -> 0% of each run, Pallas kernels for 22% -> 19%
where the time goes in v3:
time: 78.2 us; the launch traced here: 77.4 us
  Pallas kernels  26.6 us (34%)
  blocking collectives  23.4 us (30%)
  starting transfers between devices  12.3 us (16%)
  waiting for transfers between devices  11 us (14%)
  local copies, waits for them, and re-layouts  3.28 us (4%)
  other arithmetic  0.8 us (1%)
    all_to_all x1, blocking collectives, local(): lax.all_to_all(chip, ('z', 'c', 'x', 'y'), 0, 0, axis_index_groups=sums_g...  23.4 us
    all_to_all x1, starting transfers between devices, local(): mine = lax.all_to_all(everyone, CHIPS, 0, 0).reshape(HALF, N)  11.5 us
    all_to_all x1, waiting for transfers between devices, local(): mine = lax.all_to_all(everyone, CHIPS, 0, 0).reshape(HALF, N)  11 us
    pallas_call x1, Pallas kernels, prepare(): pl.pallas_call(prepare_kernel, grid=(P_DEV,), in_specs=[SMEM, SMEM, SMEM,...  7.73 us
    pallas_call x1, Pallas kernels, send_sums(): pl.pallas_call(send_kernel, in_specs=[VMEM] * 6, out_specs=VMEM, out_shap...  6.66 us
    pallas_call x1, Pallas kernels, keep_sums(): pl.pallas_call(keep_sums_kernel, in_specs=[VMEM] * 6, out_specs=VMEM, out...  4.52 us
    pallas_call x1, Pallas kernels, keep_coeff(): pl.pallas_call(keep_coeff_kernel, in_specs=[VMEM] * 4, out_specs=VMEM, ou...  4.5 us
    pallas_call x1, Pallas kernels, first_part(): pl.pallas_call(first_kernel, in_specs=[VMEM, VMEM], out_specs=VMEM, out_s...  2.35 us
  transfers between devices with their start and end apart: 3, of which 1 were waited for; matrix products, arithmetic and copies ran while one was open for 0% of the time, Pallas kernels for 19%

profile of v3, /device:TPU:0, one launch (start us, length us, event | category | flops | bytes accessed | tf_op | source)
XLA Modules:
  0.0 77.4 jit_solution(10155936428696502443)
XLA Ops:
  0.0 0.0 copy-start.2
  0.0 0.0 copy-start.3
  0.0 0.8 %reverse_select_fusion = bf16[8,2,4,128]{3,0,1,2:T(8,128)(2,1)S(1)} fusion(bf16[8,2,4,128]{3,0,1,2:T(8,128)(2,1)} %bitcast.13, pred[]{:T(512)S(6)} %eq.3), kind=kLoop, calls=%fused_computation | loop fusion | flops 8192 | bytes 32769 | tf_op jit(solution)/shard_map/jit(_where)/select_n | solution.py:201
  0.8 1.2 %broadcast_in_dim.11 = bf16[64,8,1024]{2,1,0:T(8,128)(2,1)} broadcast(bf16[8,1024]{1,0:T(8,128)(2,1)S(1)} %bitcast.12), dimensions={1,2} | broadcast | bytes 1064960 | tf_op jit(solution)/shard_map/broadcast_in_dim | solution.py:202
  2.0 11.5 %all-to-all-start = ((bf16[64,8,1024]{2,1,0:T(8,128)(2,1)}), bf16[64,8,1024]{2,1,0:T(8,128)(2,1)S(1)}, u32[]{:S(2)}, u32[]{:S(2)}) async-start(bf16[64,8,1024]{2,1,0:T(8,128)(2,1)} %broadcast_in_dim.11), calls=%async_computation | async-start | bytes 2097152 | tf_op jit(solution)/shard_map/all_to_all | solution.py:203
  13.5 0.0 copy-done.2
  13.5 0.0 copy-done.3
  13.5 7.7 %shard_map.46 = (bf16[512,2048]{1,0:T(8,128)(2,1)}, bf16[512,2048]{1,0:T(8,128)(2,1)}, bf16[512,2048]{1,0:T(8,128)(2,1)}, bf16[512,2048]{1,0:T(8,128)(2,1)}) custom-call(s32[1]{0:T(128)} %bitcast.5.place, s32[8]{0:T(128)S(1)} %copy-done.3, s32[4,8,8]{2,1,0:T(8,128)S(1)} %copy-done.2, bf16[4,1024,1024]{2,1,0:T(8,128)(2,1)} %aux.1), custom_call_target="tpu_custom_call" | custom-call | bytes 16777216 | tf_op jit(solution)/shard_map/pallas_call | solution.py:60
  21.3 11.0 %all-to-all-done = bf16[64,8,1024]{2,1,0:T(8,128)(2,1)S(1)} async-done(((bf16[64,8,1024]{2,1,0:T(8,128)(2,1)}), bf16[64,8,1024]{2,1,0:T(8,128)(2,1)S(1)}, u32[]{:S(2)}, u32[]{:S(2)}) %all-to-all-start) | async-done | bytes 1048608 | tf_op jit(solution)/shard_map/all_to_all | solution.py:203
  32.2 0.0 collective-permute-start
  32.2 0.0 copy-start
  32.2 1.6 %copy-done = bf16[512,2048]{1,0:T(8,128)(2,1)S(1)} copy-done((bf16[512,2048]{1,0:T(8,128)(2,1)S(1)}, bf16[512,2048]{1,0:T(8,128)(2,1)}, u32[]{:S(2)}) %copy-start) | copy-done | bytes 2097176
  33.8 0.0 copy-start.4
  33.8 0.0 copy-start.5
  33.8 0.0 copy-start.6
  33.8 2.3 %shard_map.48.part = f32[512,4096]{1,0:T(8,128)S(1)} custom-call(bf16[512,2048]{1,0:T(8,128)(2,1)S(1)} %copy-done, bf16[512,1024]{1,0:T(8,128)(2,1)S(1)} %bitcast.9), custom_call_target="tpu_custom_call" | custom-call | flops 2147483648 | tf_op jit(solution)/shard_map/pallas_call | solution.py:90
  36.2 0.0 collective-permute-done.theirs
  36.2 0.0 copy-done.4
  36.2 0.0 copy-done.5
  36.2 0.5 copy-done.6
  36.7 6.7 %shard_map.49 = f32[4,1024,128]{2,1,0:T(8,128)S(1)} custom-call(bf16[512,2048]{1,0:T(8,128)(2,1)S(1)} %copy-done, bf16[512,2048]{1,0:T(8,128)(2,1)S(1)} %copy-done.4, bf16[512,2048]{1,0:T(8,128)(2,1)S(1)} %copy-done.5, bf16[512,2048]{1,0:T(8,128)(2,1)S(1)} %copy-done.6, bf16[512,1024]{1,0:T(8,128)(2,1)S(1)} %collective-permute-done.theirs, ...), custom_call_target="tpu_custom_call" | custom-call | flops 6442450944 | tf_op jit(solution)/shard_map/pallas_call | solution.py:128
  43.3 0.0 copy-start.1
  43.4 0.8 collective-permute-start.1
  44.1 4.5 %shard_map.47.coeff = bf16[512,4096]{1,0:T(8,128)(2,1)S(1)} custom-call(bf16[512,2048]{1,0:T(8,128)(2,1)S(1)} %copy-done.5, bf16[512,2048]{1,0:T(8,128)(2,1)S(1)} %copy-done.6, bf16[512,1024]{1,0:T(8,128)(2,1)S(1)} %bitcast.10, bf16[512,1024]{1,0:T(8,128)(2,1)S(1)} %collective-permute-done.theirs), custom_call_target="tpu_custom_call" | custom-call | flops 4294967296 | tf_op jit(solution)/shard_map/pallas_call | solution.py:148
  48.6 0.0 collective-permute-done.1.got
  48.6 0.0 copy-done.1
  48.6 4.5 %shard_map.50 = bf16[4,1024,128]{2,1,0:T(8,128)(2,1)S(1)} custom-call(bf16[512,2048]{1,0:T(8,128)(2,1)S(1)} %copy-done.1, bf16[512,2048]{1,0:T(8,128)(2,1)S(1)} %copy-done.4, bf16[512,2048]{1,0:T(8,128)(2,1)S(1)} %copy-done.5, bf16[512,2048]{1,0:T(8,128)(2,1)S(1)} %copy-done.6, bf16[512,4096]{1,0:T(8,128)(2,1)S(1)} %shard_map.47.coeff, ...), custom_call_target="tpu_custom_call" | custom-call | flops 4294967296 | tf_op jit(solution)/shard_map/pallas_call | solution.py:166
  53.2 23.4 %all_to_all.10.parts = bf16[64,64,128]{2,1,0:T(8,128)(2,1)S(1)} all-to-all(bf16[64,64,128]{2,1,0:T(8,128)(2,1)S(1)} %bitcast.11), channel_id=1, replica_groups={{2,3,6,7,10,11,14,15,0,1,4,5,8,9,12,13,34,35,38,39,42,43,46,47,32,33,36..., dimensions={0} | all-to-all | bytes 2097152 | tf_op jit(solution)/shard_map/all_to_all | solution.py:210
  76.6 0.8 %shard_map.51 = f32[64,128]{1,0:T(8,128)} custom-call(bf16[64,64,128]{2,1,0:T(8,128)(2,1)S(1)} %all_to_all.10.parts), custom_call_target="tpu_custom_call" | custom-call | tf_op jit(solution)/shard_map/pallas_call | solution.py:181
  (1 shorter events, 0.0 us)
Async XLA Ops:
  0.0 13.5 %copy-start.2 = (s32[4,8,8]{2,1,0:T(8,128)S(1)}, s32[4,8,8]{2,1,0:T(8,128)}, u32[]{:S(2)}) copy-start(s32[4,8,8]{2,1,0:T(8,128)} %pattern.1) | copy-start | bytes 3076
  0.0 13.5 %copy-start.3 = (s32[8]{0:T(128)S(1)}, s32[8]{0:T(128)}, u32[]{:S(2)}) copy-start(s32[8]{0:T(128)} %sizes.1) | copy-start | bytes 100
  2.0 30.2 %all-to-all-start = ((bf16[64,8,1024]{2,1,0:T(8,128)(2,1)}), bf16[64,8,1024]{2,1,0:T(8,128)(2,1)S(1)}, u32[]{:S(2)}, u32[]{:S(2)}) async-start(bf16[64,8,1024]{2,1,0:T(8,128)(2,1)} %broadcast_in_dim.11), calls=%async_computation | async-start | bytes 2097152 | tf_op jit(solution)/shard_map/all_to_all | solution.py:203
  32.2 4.0 %collective-permute-start = (bf16[512,1024]{1,0:T(8,128)(2,1)S(1)}, bf16[512,1024]{1,0:T(8,128)(2,1)S(1)}, u32[]{:S(2)}, u32[]{:S(2)}) collective-permute-start(bf16[512,1024]{1,0:T(8,128)(2,1)S(1)} %bitcast.8), channel_id=1, source_target_pairs={{0,16},{16,0},{1,17},{17,1},{2,18},{18,2},{3,19},{19,3},{4,20},{20... | collective-permute-start | bytes 3145736 | tf_op jit(solution)/shard_map/ppermute | solution.py:205
  32.2 1.6 %copy-start = (bf16[512,2048]{1,0:T(8,128)(2,1)S(1)}, bf16[512,2048]{1,0:T(8,128)(2,1)}, u32[]{:S(2)}) copy-start(bf16[512,2048]{1,0:T(8,128)(2,1)} %get-tuple-element.18.send_own) | copy-start | bytes 6291460
  33.8 2.4 %copy-start.4 = (bf16[512,2048]{1,0:T(8,128)(2,1)S(1)}, bf16[512,2048]{1,0:T(8,128)(2,1)}, u32[]{:S(2)}) copy-start(bf16[512,2048]{1,0:T(8,128)(2,1)} %get-tuple-element.19.send_other) | copy-start | bytes 6291460
  33.8 2.4 %copy-start.5 = (bf16[512,2048]{1,0:T(8,128)(2,1)S(1)}, bf16[512,2048]{1,0:T(8,128)(2,1)}, u32[]{:S(2)}) copy-start(bf16[512,2048]{1,0:T(8,128)(2,1)} %get-tuple-element.20.keep_own) | copy-start | bytes 6291460
  33.8 2.9 %copy-start.6 = (bf16[512,2048]{1,0:T(8,128)(2,1)S(1)}, bf16[512,2048]{1,0:T(8,128)(2,1)}, u32[]{:S(2)}) copy-start(bf16[512,2048]{1,0:T(8,128)(2,1)} %get-tuple-element.21.keep_other) | copy-start | bytes 6291460
  43.3 5.3 %copy-start.1 = (bf16[512,2048]{1,0:T(8,128)(2,1)S(1)}, bf16[512,2048]{1,0:T(8,128)(2,1)}, u32[]{:S(2)}) copy-start(bf16[512,2048]{1,0:T(8,128)(2,1)} %get-tuple-element.18.send_own) | copy-start | bytes 6291460
  43.4 5.3 %collective-permute-start.1 = (f32[4,1024,128]{2,1,0:T(8,128)S(1)}, f32[4,1024,128]{2,1,0:T(8,128)S(1)}, u32[]{:S(2)}, u32[]{:S(2)}) collective-permute-start(f32[4,1024,128]{2,1,0:T(8,128)S(1)} %shard_map.49), channel_id=1, source_target_pairs={{0,16},{16,0},{1,17},{17,1},{2,18},{18,2},{3,19},{19,3},{4,20},{20... | collective-permute-start | bytes 6291464 | tf_op jit(solution)/shard_map/ppermute | solution.py:207

commit v4 on v3

--- a/solution.py
+++ b/solution.py
@@ -52,17 +52,18 @@
         for j, k in enumerate(order):
             value = aux[0, block(b), block(k)] * (rows * cols[j]).astype(BF16)
             other, to = divmod(j, NB // 2)
-            outs[half][other][at * BS:(at + 1) * BS, to * BS:(to + 1) * BS] = value
+            which = p if half and not other else 0
+            outs[half][other][which, at * BS:(at + 1) * BS, to * BS:(to + 1) * BS] = value
 
 
 def prepare(place, sizes, pattern, aux):
-    quarter = pl.BlockSpec((HALF, HALF), lambda p: (0, p))
+    quarter = pl.BlockSpec((1, HALF, HALF), lambda p: (p, 0, 0))
     return pl.pallas_call(
         prepare_kernel,
         grid=(P_DEV,),
         in_specs=[SMEM, SMEM, SMEM, pl.BlockSpec((1, N, N), lambda p: (p, 0, 0))],
-        out_specs=[quarter] * 4,
-        out_shape=[pltpu.HBM((HALF, WIDE // 2), BF16)] * 4,
+        out_specs=[VMEM] + [quarter] * 3,
+        out_shape=[jax.ShapeDtypeStruct((P_DEV, HALF, HALF), BF16)] + [pltpu.HBM((P_DEV, HALF, HALF), BF16)] * 3,
         compiler_params=params(48),
         cost_estimate=pl.CostEstimate(flops=0, bytes_accessed=2 * 2 * N * WIDE, transcendentals=0),
     )(place, sizes, pattern, aux)
@@ -76,14 +77,10 @@
         yield slice(t * TILE, (t + 1) * TILE), slice(swapped, swapped + TILE), slice(at, at + TILE)
 
 
-def slab(p):
-    return slice(p * HALF, (p + 1) * HALF)
-
-
 def first_kernel(send_own, mine, part):
     for p in range(P_DEV):
         for s, _, at in tiles(p):
-            part[:, at] = lax.dot_general(send_own[:, slab(p)], mine[:, s], NN, preferred_element_type=F32)
+            part[:, at] = lax.dot_general(send_own[p], mine[:, s], NN, preferred_element_type=F32)
 
 
 def first_part(send_own, mine):
@@ -101,8 +98,8 @@
     send_own, send_other, keep_own, keep_other = aux
     rows = jnp.concatenate(
         [
-            jnp.concatenate([send_own[...], send_other[...]], axis=1),
-            jnp.concatenate([keep_own[...], keep_other[...]], axis=1),
+            jnp.concatenate([quarter[p] for quarter in half for p in range(P_DEV)], axis=1)
+            for half in ((send_own, send_other), (keep_own, keep_other))
         ],
         axis=0,
     )
@@ -115,7 +112,7 @@
 def send_kernel(send_own, send_other, keep_own, keep_other, theirs, part, out, coeff):
     for p in range(P_DEV):
         for s, swapped, at in tiles(p):
-            value = lax.dot_general(send_other[:, slab(p)], theirs[:, swapped], NN, preferred_element_type=F32)
+            value = lax.dot_general(send_other[p], theirs[:, swapped], NN, preferred_element_type=F32)
             coeff[:, at] = (part[:, at] + value).astype(BF16)
 
     def store(z, value):
@@ -138,7 +135,7 @@
 
 def keep_coeff_kernel(keep_own, keep_other, mine, theirs, coeff):
     for p in range(P_DEV):
-        rows = jnp.concatenate([keep_own[:, slab(p)], keep_other[:, slab(p)]], axis=1)
+        rows = jnp.concatenate([keep_own[p], keep_other[p]], axis=1)
         for s, swapped, at in tiles(p):
             dens = jnp.concatenate([mine[:, s], theirs[:, swapped]], axis=0)
             coeff[:, at] = lax.dot_general(rows, dens, NN, preferred_element_type=F32).astype(BF16)

time: 78.2 us -> 76.8 us (0.982)
  local copies, waits for them, and re-layouts: 3.28 us -> 1.32 us
  waiting for transfers between devices: 11 us -> 12.2 us
  Pallas kernels: 26.6 us -> 25.7 us
    unnamed x14 -> x10, local copies, waits for them, and re-layouts: 2.09 us -> 0.2 us
    all_to_all x1, waiting for transfers between devices: 11 us -> 11.9 us  [local(): mine = lax.all_to_all(everyone, CHIPS, 0, 0).reshape(HALF, N)]
    pallas_call x1, Pallas kernels: 7.73 us -> 6.82 us  [prepare(): pl.pallas_call(prepare_kernel, grid=(P_DEV,), in_specs=[SMEM, SMEM, SMEM,...]
  transfers between devices with their start and end apart: 3 -> 3, of which waited for: 1 -> 2; matrix products, arithmetic and copies ran while one was open for 0% -> 0% of each run, Pallas kernels for 19% -> 18%
where the time goes in v4:
time: 76.8 us; the launch traced here: 75.8 us
  Pallas kernels  25.7 us (33%)
  blocking collectives  23.9 us (31%)
  waiting for transfers between devices  12.2 us (16%)
  starting transfers between devices  11.8 us (15%)
  local copies, waits for them, and re-layouts  1.32 us (2%)
  other arithmetic  0.8 us (1%)
    all_to_all x1, blocking collectives, local(): lax.all_to_all(chip, ('z', 'c', 'x', 'y'), 0, 0, axis_index_groups=sums_g...  23.9 us
    all_to_all x1, waiting for transfers between devices, local(): mine = lax.all_to_all(everyone, CHIPS, 0, 0).reshape(HALF, N)  11.9 us
    all_to_all x1, starting transfers between devices, local(): mine = lax.all_to_all(everyone, CHIPS, 0, 0).reshape(HALF, N)  11.5 us
    pallas_call x1, Pallas kernels, prepare(): pl.pallas_call(prepare_kernel, grid=(P_DEV,), in_specs=[SMEM, SMEM, SMEM,...  6.82 us
    pallas_call x1, Pallas kernels, send_sums(): pl.pallas_call(send_kernel, in_specs=[VMEM] * 6, out_specs=VMEM, out_shap...  6.69 us
    pallas_call x1, Pallas kernels, keep_sums(): pl.pallas_call(keep_sums_kernel, in_specs=[VMEM] * 6, out_specs=VMEM, out...  4.51 us
    pallas_call x1, Pallas kernels, keep_coeff(): pl.pallas_call(keep_coeff_kernel, in_specs=[VMEM] * 4, out_specs=VMEM, ou...  4.5 us
    pallas_call x1, Pallas kernels, first_part(): pl.pallas_call(first_kernel, in_specs=[VMEM, VMEM], out_specs=VMEM, out_s...  2.35 us
  transfers between devices with their start and end apart: 3, of which 2 were waited for; matrix products, arithmetic and copies ran while one was open for 0% of the time, Pallas kernels for 18%

profile of v4, /device:TPU:0, one launch (start us, length us, event | category | flops | bytes accessed | tf_op | source)
XLA Modules:
  0.0 75.8 jit_solution(16930096815688235235)
XLA Ops:
  0.0 0.0 copy-start
  0.0 0.0 copy-start.1
  0.0 0.8 %reverse_select_fusion = bf16[8,2,4,128]{3,0,1,2:T(8,128)(2,1)S(1)} fusion(bf16[8,2,4,128]{3,0,1,2:T(8,128)(2,1)} %bitcast.13, pred[]{:T(512)S(6)} %eq.3), kind=kLoop, calls=%fused_computation | loop fusion | flops 8192 | bytes 32769 | tf_op jit(solution)/shard_map/jit(_where)/select_n | solution.py:198
  0.8 1.1 %broadcast_in_dim.11 = bf16[64,8,1024]{2,1,0:T(8,128)(2,1)} broadcast(bf16[8,1024]{1,0:T(8,128)(2,1)S(1)} %bitcast.12), dimensions={1,2} | broadcast | bytes 1064960 | tf_op jit(solution)/shard_map/broadcast_in_dim | solution.py:199
  1.9 11.5 %all-to-all-start = ((bf16[64,8,1024]{2,1,0:T(8,128)(2,1)}), bf16[64,8,1024]{2,1,0:T(8,128)(2,1)S(1)}, u32[]{:S(2)}, u32[]{:S(2)}) async-start(bf16[64,8,1024]{2,1,0:T(8,128)(2,1)} %broadcast_in_dim.11), calls=%async_computation | async-start | bytes 2097152 | tf_op jit(solution)/shard_map/all_to_all | solution.py:200
  13.4 0.0 copy-done
  13.4 0.0 copy-done.1
  13.5 6.8 %shard_map.46 = (bf16[4,512,512]{2,1,0:T(8,128)(2,1)S(1)}, bf16[4,512,512]{2,1,0:T(8,128)(2,1)}, bf16[4,512,512]{2,1,0:T(8,128)(2,1)}, bf16[4,512,512]{2,1,0:T(8,128)(2,1)}) custom-call(s32[1]{0:T(128)} %bitcast.5.place, s32[8]{0:T(128)S(1)} %copy-done.1, s32[4,8,8]{2,1,0:T(8,128)S(1)} %copy-done, bf16[4,1024,1024]{2,1,0:T(8,128)(2,1)} %aux.1), custom_call_target="tpu_custom_call" | custom-call | bytes 16777216 | tf_op jit(solution)/shard_map/pallas_call | solution.py:61
  20.3 11.9 %all-to-all-done = bf16[64,8,1024]{2,1,0:T(8,128)(2,1)S(1)} async-done(((bf16[64,8,1024]{2,1,0:T(8,128)(2,1)}), bf16[64,8,1024]{2,1,0:T(8,128)(2,1)S(1)}, u32[]{:S(2)}, u32[]{:S(2)}) %all-to-all-start) | async-done | bytes 1048608 | tf_op jit(solution)/shard_map/all_to_all | solution.py:200
  32.1 0.0 copy-start.2
  32.2 0.0 copy-start.3
  32.2 0.0 copy-start.4
  32.2 0.0 collective-permute-start
  32.2 2.3 %shard_map.48.part = f32[512,4096]{1,0:T(8,128)S(1)} custom-call(bf16[4,512,512]{2,1,0:T(8,128)(2,1)S(1)} %get-tuple-element.18.send_own, bf16[512,1024]{1,0:T(8,128)(2,1)S(1)} %bitcast.9), custom_call_target="tpu_custom_call" | custom-call | flops 2147483648 | tf_op jit(solution)/shard_map/pallas_call | solution.py:87
  34.5 0.3 collective-permute-done.theirs
  34.8 0.0 copy-done.2
  34.8 0.0 copy-done.3
  34.8 0.2 copy-done.4
  35.0 6.7 %shard_map.49 = f32[4,1024,128]{2,1,0:T(8,128)S(1)} custom-call(bf16[4,512,512]{2,1,0:T(8,128)(2,1)S(1)} %get-tuple-element.18.send_own, bf16[4,512,512]{2,1,0:T(8,128)(2,1)S(1)} %copy-done.2, bf16[4,512,512]{2,1,0:T(8,128)(2,1)S(1)} %copy-done.3, bf16[4,512,512]{2,1,0:T(8,128)(2,1)S(1)} %copy-done.4, bf16[512,1024]{1,0:T(8,128)(2,1)S(1)} %collective-permute-done.theirs, ...), custom_call_target="tpu_custom_call" | custom-call | flops 6442450944 | tf_op jit(solution)/shard_map/pallas_call | solution.py:125
  41.7 0.3 collective-permute-start.1
  42.0 4.5 %shard_map.47.coeff = bf16[512,4096]{1,0:T(8,128)(2,1)S(1)} custom-call(bf16[4,512,512]{2,1,0:T(8,128)(2,1)S(1)} %copy-done.3, bf16[4,512,512]{2,1,0:T(8,128)(2,1)S(1)} %copy-done.4, bf16[512,1024]{1,0:T(8,128)(2,1)S(1)} %bitcast.10, bf16[512,1024]{1,0:T(8,128)(2,1)S(1)} %collective-permute-done.theirs), custom_call_target="tpu_custom_call" | custom-call | flops 4294967296 | tf_op jit(solution)/shard_map/pallas_call | solution.py:145
  46.5 0.0 collective-permute-done.1.got
  46.5 4.5 %shard_map.50 = bf16[4,1024,128]{2,1,0:T(8,128)(2,1)S(1)} custom-call(bf16[4,512,512]{2,1,0:T(8,128)(2,1)S(1)} %get-tuple-element.18.send_own, bf16[4,512,512]{2,1,0:T(8,128)(2,1)S(1)} %copy-done.2, bf16[4,512,512]{2,1,0:T(8,128)(2,1)S(1)} %copy-done.3, bf16[4,512,512]{2,1,0:T(8,128)(2,1)S(1)} %copy-done.4, bf16[512,4096]{1,0:T(8,128)(2,1)S(1)} %shard_map.47.coeff, ...), custom_call_target="tpu_custom_call" | custom-call | flops 4294967296 | tf_op jit(solution)/shard_map/pallas_call | solution.py:163
  51.0 23.9 %all_to_all.10.parts = bf16[64,64,128]{2,1,0:T(8,128)(2,1)S(1)} all-to-all(bf16[64,64,128]{2,1,0:T(8,128)(2,1)S(1)} %bitcast.11), channel_id=1, replica_groups={{2,3,6,7,10,11,14,15,0,1,4,5,8,9,12,13,34,35,38,39,42,43,46,47,32,33,36..., dimensions={0} | all-to-all | bytes 2097152 | tf_op jit(solution)/shard_map/all_to_all | solution.py:207
  75.0 0.8 %shard_map.51 = f32[64,128]{1,0:T(8,128)} custom-call(bf16[64,64,128]{2,1,0:T(8,128)(2,1)S(1)} %all_to_all.10.parts), custom_call_target="tpu_custom_call" | custom-call | tf_op jit(solution)/shard_map/pallas_call | solution.py:178
  (1 shorter events, 0.0 us)
Async XLA Ops:
  0.0 13.4 %copy-start = (s32[4,8,8]{2,1,0:T(8,128)S(1)}, s32[4,8,8]{2,1,0:T(8,128)}, u32[]{:S(2)}) copy-start(s32[4,8,8]{2,1,0:T(8,128)} %pattern.1) | copy-start | bytes 3076
  0.0 13.4 %copy-start.1 = (s32[8]{0:T(128)S(1)}, s32[8]{0:T(128)}, u32[]{:S(2)}) copy-start(s32[8]{0:T(128)} %sizes.1) | copy-start | bytes 100
  1.9 30.2 %all-to-all-start = ((bf16[64,8,1024]{2,1,0:T(8,128)(2,1)}), bf16[64,8,1024]{2,1,0:T(8,128)(2,1)S(1)}, u32[]{:S(2)}, u32[]{:S(2)}) async-start(bf16[64,8,1024]{2,1,0:T(8,128)(2,1)} %broadcast_in_dim.11), calls=%async_computation | async-start | bytes 2097152 | tf_op jit(solution)/shard_map/all_to_all | solution.py:200
  32.1 2.7 %copy-start.2 = (bf16[4,512,512]{2,1,0:T(8,128)(2,1)S(1)}, bf16[4,512,512]{2,1,0:T(8,128)(2,1)}, u32[]{:S(2)}) copy-start(bf16[4,512,512]{2,1,0:T(8,128)(2,1)} %get-tuple-element.19.send_other) | copy-start | bytes 6291460
  32.2 2.7 %copy-start.3 = (bf16[4,512,512]{2,1,0:T(8,128)(2,1)S(1)}, bf16[4,512,512]{2,1,0:T(8,128)(2,1)}, u32[]{:S(2)}) copy-start(bf16[4,512,512]{2,1,0:T(8,128)(2,1)} %get-tuple-element.20.keep_own) | copy-start | bytes 6291460
  32.2 2.9 %copy-start.4 = (bf16[4,512,512]{2,1,0:T(8,128)(2,1)S(1)}, bf16[4,512,512]{2,1,0:T(8,128)(2,1)}, u32[]{:S(2)}) copy-start(bf16[4,512,512]{2,1,0:T(8,128)(2,1)} %get-tuple-element.21.keep_other) | copy-start | bytes 6291460
  32.2 2.7 %collective-permute-start = (bf16[512,1024]{1,0:T(8,128)(2,1)S(1)}, bf16[512,1024]{1,0:T(8,128)(2,1)S(1)}, u32[]{:S(2)}, u32[]{:S(2)}) collective-permute-start(bf16[512,1024]{1,0:T(8,128)(2,1)S(1)} %bitcast.8), channel_id=1, source_target_pairs={{0,16},{16,0},{1,17},{17,1},{2,18},{18,2},{3,19},{19,3},{4,20},{20... | collective-permute-start | bytes 3145736 | tf_op jit(solution)/shard_map/ppermute | solution.py:202
  41.7 4.8 %collective-permute-start.1 = (f32[4,1024,128]{2,1,0:T(8,128)S(1)}, f32[4,1024,128]{2,1,0:T(8,128)S(1)}, u32[]{:S(2)}, u32[]{:S(2)}) collective-permute-start(f32[4,1024,128]{2,1,0:T(8,128)S(1)} %shard_map.49), channel_id=1, source_target_pairs={{0,16},{16,0},{1,17},{17,1},{2,18},{18,2},{3,19},{19,3},{4,20},{20... | collective-permute-start | bytes 6291464 | tf_op jit(solution)/shard_map/ppermute | solution.py:204

commit v5 on v4

--- a/solution.py
+++ b/solution.py
@@ -1,3 +1,5 @@
+import functools
+
 import jax
 import jax.numpy as jnp
 from jax import lax
@@ -35,6 +37,11 @@
     return [2 * z + core for z in range(NB // 2)] + [2 * z + 1 - core for z in range(NB // 2)]
 
 
+def row_order(core, odd):
+    zs = (1 - odd, 3 - odd, odd, odd + 2)
+    return [2 * z + core for z in zs] + [2 * z + 1 - core for z in zs]
+
+
 def block(index):
     return pl.ds(pl.multiple_of(index * BS, BS), BS)
 
@@ -44,9 +51,10 @@
     lane = lax.broadcasted_iota(jnp.int32, (1, BS), 1)
     row = lax.broadcasted_iota(jnp.int32, (BS, 1), 0)
     order = core_order(place[0])
+    rows_order = row_order(place[0], place[1])
     cols = [((lane < sizes[b]) & (pattern[p, b, b] > 0)).astype(F32) for b in order]
     outs = ((keep_own, keep_other), (send_own, send_other))
-    for i, b in enumerate(order):
+    for i, b in enumerate(rows_order):
         rows = ((row < sizes[b]) & (pattern[p, b, b] > 0)).astype(F32)
         half, at = divmod(i, NB // 2)
         for j, k in enumerate(order):
@@ -94,80 +102,129 @@
     )(send_own, mine)
 
 
-def half_sums(aux, coeff, store):
-    send_own, send_other, keep_own, keep_other = aux
+def part_sums(aux, coeff, store):
     rows = jnp.concatenate(
         [
             jnp.concatenate([quarter[p] for quarter in half for p in range(P_DEV)], axis=1)
-            for half in ((send_own, send_other), (keep_own, keep_other))
+            for half in (aux[:2], aux[2:])
         ],
         axis=0,
     )
-    for t in range(HALF // TILE):
-        value = lax.dot_general(rows, coeff[t * TILE:(t + 1) * TILE, :], NT, preferred_element_type=F32)
-        for h in range(TILE // BS):
-            store(t * (TILE // BS) + h, value[:, h * BS:(h + 1) * BS])
-
-
-def send_kernel(send_own, send_other, keep_own, keep_other, theirs, part, out, coeff):
+    value = lax.dot_general(rows, coeff[...], NT, preferred_element_type=F32)
+    for h in range(TILE // BS):
+        store(h, value[:, h * BS:(h + 1) * BS])
+
+
+def part_rows(far):
+    return slice(TILE, 2 * TILE) if far else slice(0, TILE)
+
+
+def send_kernel(far, send_own, send_other, keep_own, keep_other, theirs, part, out, coeff):
+    rows = part_rows(far)
     for p in range(P_DEV):
         for s, swapped, at in tiles(p):
-            value = lax.dot_general(send_other[p], theirs[:, swapped], NN, preferred_element_type=F32)
-            coeff[:, at] = (part[:, at] + value).astype(BF16)
-
-    def store(z, value):
-        out[z] = value
-
-    half_sums((send_own, send_other, keep_own, keep_other), coeff, store)
-
-
-def send_sums(aux, theirs, part):
-    return pl.pallas_call(
-        send_kernel,
+            value = lax.dot_general(send_other[p, rows], theirs[:, swapped], NN, preferred_element_type=F32)
+            coeff[:, at] = (part[rows, at] + value).astype(BF16)
+
+    def store(h, value):
+        out[h] = value
+
+    part_sums((send_own, send_other, keep_own, keep_other), coeff, store)
+
+
+def send_sums(far, aux, theirs, part):
+    return pl.pallas_call(
+        functools.partial(send_kernel, far),
         in_specs=[VMEM] * 6,
         out_specs=VMEM,
-        out_shape=jax.ShapeDtypeStruct((NB // 2, N, BS), F32),
-        scratch_shapes=[pltpu.VMEM((HALF, WIDE), BF16)],
-        compiler_params=params(20),
-        cost_estimate=cost(1.5),
+        out_shape=jax.ShapeDtypeStruct((TILE // BS, N, BS), F32),
+        scratch_shapes=[pltpu.VMEM((TILE, WIDE), BF16)],
+        compiler_params=params(20),
+        cost_estimate=cost(0.75),
     )(*aux, theirs, part)
 
 
-def keep_coeff_kernel(keep_own, keep_other, mine, theirs, coeff):
+def keep_coeff(far, keep_own, keep_other, mine, theirs, coeff):
     for p in range(P_DEV):
-        rows = jnp.concatenate([keep_own[p], keep_other[p]], axis=1)
+        rows = jnp.concatenate([keep_own[p, part_rows(far)], keep_other[p, part_rows(far)]], axis=1)
         for s, swapped, at in tiles(p):
             dens = jnp.concatenate([mine[:, s], theirs[:, swapped]], axis=0)
             coeff[:, at] = lax.dot_general(rows, dens, NN, preferred_element_type=F32).astype(BF16)
 
 
-def keep_coeff(aux, mine, theirs):
-    return pl.pallas_call(
-        keep_coeff_kernel,
-        in_specs=[VMEM] * 4,
-        out_specs=VMEM,
-        out_shape=jax.ShapeDtypeStruct((HALF, WIDE), BF16),
+def other_order(got, h):
+    return jnp.concatenate([got[h, HALF:, :], got[h, :HALF, :]], axis=0)
+
+
+def near_kernel(place, send_own, send_other, keep_own, keep_other, mine, theirs, got, up, down, coeff):
+    keep_coeff(False, keep_own, keep_other, mine, theirs, coeff)
+    first_up = (place[2] == 0) | (place[2] == 3)
+
+    def store(h, value):
+        value = (value + other_order(got, h)).astype(BF16)
+        goes_up = first_up if h == 0 else jnp.logical_not(first_up)
+
+        @pl.when(goes_up)
+        def _():
+            up[...] = value
+
+        @pl.when(jnp.logical_not(goes_up))
+        def _():
+            down[...] = value
+
+    part_sums((send_own, send_other, keep_own, keep_other), coeff, store)
+
+
+def near_sums(place, aux, mine, theirs, got):
+    return pl.pallas_call(
+        near_kernel,
+        in_specs=[SMEM] + [VMEM] * 7,
+        out_specs=[VMEM, VMEM],
+        out_shape=[jax.ShapeDtypeStruct((N, BS), BF16)] * 2,
+        scratch_shapes=[pltpu.VMEM((TILE, WIDE), BF16)],
         compiler_params=params(20),
         cost_estimate=cost(1),
-    )(aux[2], aux[3], mine, theirs)
-
-
-def keep_sums_kernel(send_own, send_other, keep_own, keep_other, coeff, got, out):
-    def store(z, value):
-        out[z] = (value + jnp.concatenate([got[z, HALF:, :], got[z, :HALF, :]], axis=0)).astype(BF16)
-
-    half_sums((send_own, send_other, keep_own, keep_other), coeff, store)
-
-
-def keep_sums(aux, coeff, got):
-    return pl.pallas_call(
-        keep_sums_kernel,
-        in_specs=[VMEM] * 6,
-        out_specs=VMEM,
-        out_shape=jax.ShapeDtypeStruct((NB // 2, N, BS), BF16),
+    )(place, *aux, mine, theirs, got)
+
+
+def far_kernel(send_own, send_other, keep_own, keep_other, mine, theirs, got, out, coeff):
+    keep_coeff(True, keep_own, keep_other, mine, theirs, coeff)
+
+    def store(h, value):
+        out[h] = value + other_order(got, h)
+
+    part_sums((send_own, send_other, keep_own, keep_other), coeff, store)
+
+
+def far_sums(aux, mine, theirs, got):
+    return pl.pallas_call(
+        far_kernel,
+        in_specs=[VMEM] * 7,
+        out_specs=VMEM,
+        out_shape=jax.ShapeDtypeStruct((TILE // BS, N, BS), F32),
+        scratch_shapes=[pltpu.VMEM((TILE, WIDE), BF16)],
         compiler_params=params(20),
         cost_estimate=cost(1),
-    )(*aux, coeff, got)
+    )(*aux, mine, theirs, got)
+
+
+def join_kernel(place, far, low, high, out):
+    for i, j in enumerate((1, 0, 3, 2)):
+        to, at = slice(i * TILE, (i + 1) * TILE), slice(j * TILE, (j + 1) * TILE)
+        both = low[at, :].astype(F32) + high[at, :].astype(F32)
+        for h in range(TILE // BS):
+            own = (place[2] // 2 == h).astype(F32)
+            out[h, to, :] = (far[h, to, :] + both * own).astype(BF16)
+
+
+def join(place, far, low, high):
+    return pl.pallas_call(
+        join_kernel,
+        in_specs=[SMEM, VMEM, VMEM, VMEM],
+        out_specs=VMEM,
+        out_shape=jax.ShapeDtypeStruct((TILE // BS, N, BS), BF16),
+        compiler_params=params(20),
+    )(place, far, low, high)
 
 
 def finish_kernel(parts, out):
@@ -185,25 +242,40 @@
 
 
 def sums_groups():
+    def second(core, odd):
+        order = row_order(core, odd)
+        return order[NB // 2:] + order[:NB // 2]
+
     return [
-        [(z * 2 + core) * 16 + 2 * b + h for z in range(NB // 2) for b in core_order(1 - core) for h in range(2)]
+        [(z * 2 + core) * 16 + 2 * b + h for z in (odd, odd + 2) for b in second(core, odd) for h in range(2)]
+        for odd in range(2)
         for core in range(2)
     ]
 
 
 def local(aux_ints, density, pattern, block_sizes):
     core = lax.axis_index("c")
-    swap = [(0, 1), (1, 0)]
+    z = lax.axis_index("z")
+    place = jnp.stack([core, lax.rem(z, 2), z])
+
+    def swap(array):
+        return lax.ppermute(array, "c", [(0, 1), (1, 0)])
+
     blocks = density.reshape(ROWS, NB // 2, 2, BS).swapaxes(1, 2)
     blocks = jnp.where(core == 0, blocks, blocks[:, ::-1]).reshape(ROWS, N)
     everyone = jnp.broadcast_to(blocks[None], (CHIP_COUNT, ROWS, N))
     mine = lax.all_to_all(everyone, CHIPS, 0, 0).reshape(HALF, N)
-    mine, aux = lax.optimization_barrier((mine, prepare(core[None], block_sizes, pattern, aux_ints)))
-    theirs = lax.ppermute(mine, "c", swap)
+    mine, aux = lax.optimization_barrier((mine, prepare(place, block_sizes, pattern, aux_ints)))
+    theirs = swap(mine)
     part = first_part(aux[0], mine)
-    got = lax.ppermute(send_sums(aux, theirs, part), "c", swap)
-    chip = keep_sums(aux, keep_coeff(aux, mine, theirs), got)
-    chip = chip.reshape(CHIP_COUNT, BS // 2, BS)
+    got = swap(send_sums(False, aux, theirs, part))
+    up, down = near_sums(place, aux, mine, theirs, got)
+    low = lax.ppermute(up, "z", [(i, (i + 1) % 4) for i in range(4)])
+    high = lax.ppermute(down, "z", [(i, (i - 1) % 4) for i in range(4)])
+    got = swap(send_sums(True, aux, theirs, part))
+    far = far_sums(aux, mine, theirs, got)
+    chip = join(place, far, low, high)
+    chip = chip.reshape(CHIP_COUNT // 2, BS // 2, BS)
     parts = lax.all_to_all(chip, ("z", "c", "x", "y"), 0, 0, axis_index_groups=sums_groups())
     return finish(parts).T
 

time: 76.8 us -> 76.3 us (level)
  blocking collectives: 23.9 us -> 16.8 us
  starting transfers between devices: 11.8 us -> 15.6 us
  Pallas kernels: 25.7 us -> 27.3 us
  waiting for transfers between devices: 12.2 us -> 13.8 us
    all_to_all x1, blocking collectives: 23.9 us -> 16.8 us  [local(): lax.all_to_all(chip, ('z', 'c', 'x', 'y'), 0, 0, axis_index_groups=sums_g...]
    ppermute x2 -> x5, starting transfers between devices: 0.31 us -> 4.15 us  [the longest x1 2.96 us: local(): high = lax.ppermute(down, 'z', [(i, (i - 1) % 4) for i in range(4)])]
    pallas_call x3 -> x5, Pallas kernels: 15.7 us -> 17.4 us  [the longest x2 6.97 us: send_sums(): pl.pallas_call(functools.partial(send_kernel, far), in_specs=[VMEM] * 6,...]
    ppermute x2 -> x5, waiting for transfers between devices: 0.31 us -> 1.97 us  [the longest x1 1.66 us: local(): low = lax.ppermute(up, 'z', [(i, (i + 1) % 4) for i in range(4)])]
  transfers between devices with their start and end apart: 3 -> 6, of which waited for: 2 -> 3; matrix products, arithmetic and copies ran while one was open for 0% -> 0% of each run, Pallas kernels for 18% -> 30%
where the time goes in v5:
time: 76.3 us; the launch traced here: 75.8 us
  Pallas kernels  27.3 us (36%)
  blocking collectives  16.8 us (22%)
  starting transfers between devices  15.6 us (20%)
  waiting for transfers between devices  13.8 us (18%)
  local copies, waits for them, and re-layouts  1.33 us (2%)
  other arithmetic  0.88 us (1%)
    all_to_all x1, blocking collectives, local(): lax.all_to_all(chip, ('z', 'c', 'x', 'y'), 0, 0, axis_index_groups=sums_g...  16.8 us
    all_to_all x1, waiting for transfers between devices, local(): mine = lax.all_to_all(everyone, CHIPS, 0, 0).reshape(HALF, N)  11.8 us
    all_to_all x1, starting transfers between devices, local(): mine = lax.all_to_all(everyone, CHIPS, 0, 0).reshape(HALF, N)  11.5 us
    pallas_call x2, Pallas kernels, send_sums(): pl.pallas_call(functools.partial(send_kernel, far), in_specs=[VMEM] * 6,...  6.97 us
    pallas_call x1, Pallas kernels, prepare(): pl.pallas_call(prepare_kernel, grid=(P_DEV,), in_specs=[SMEM, SMEM, SMEM,...  6.84 us
    pallas_call x1, Pallas kernels, near_sums(): pl.pallas_call(near_kernel, in_specs=[SMEM] + [VMEM] * 7, out_specs=[VMEM...  5.2 us
    pallas_call x1, Pallas kernels, far_sums(): pl.pallas_call(far_kernel, in_specs=[VMEM] * 7, out_specs=VMEM, out_shape...  4.56 us
    ppermute x1, starting transfers between devices, local(): high = lax.ppermute(down, 'z', [(i, (i - 1) % 4) for i in range(4)])  2.96 us
  transfers between devices with their start and end apart: 6, of which 3 were waited for; matrix products, arithmetic and copies ran while one was open for 0% of the time, Pallas kernels for 30%

profile of v5, /device:TPU:0, one launch (start us, length us, event | category | flops | bytes accessed | tf_op | source)
XLA Modules:
  0.0 75.8 jit_solution(3942587346431909532)
XLA Ops:
  0.0 0.0 copy-start.4
  0.0 0.0 copy-start.3
  0.0 0.8 %reverse_select_fusion = bf16[8,2,4,128]{3,0,1,2:T(8,128)(2,1)S(1)} fusion(bf16[8,2,4,128]{3,0,1,2:T(8,128)(2,1)} %bitcast.16, pred[]{:T(512)S(6)} %eq.3), kind=kLoop, calls=%fused_computation | loop fusion | flops 8192 | bytes 32769 | tf_op jit(solution)/shard_map/jit(_where)/select_n | solution.py:265
  0.8 1.1 %broadcast_in_dim.8 = bf16[64,8,1024]{2,1,0:T(8,128)(2,1)} broadcast(bf16[8,1024]{1,0:T(8,128)(2,1)S(1)} %bitcast.15), dimensions={1,2} | broadcast | bytes 1064960 | tf_op jit(solution)/shard_map/broadcast_in_dim | solution.py:266
  1.9 11.5 %all-to-all-start = ((bf16[64,8,1024]{2,1,0:T(8,128)(2,1)}), bf16[64,8,1024]{2,1,0:T(8,128)(2,1)S(1)}, u32[]{:S(2)}, u32[]{:S(2)}) async-start(bf16[64,8,1024]{2,1,0:T(8,128)(2,1)} %broadcast_in_dim.8), calls=%async_computation | async-start | bytes 2097152 | tf_op jit(solution)/shard_map/all_to_all | solution.py:267
  13.4 0.1 pad_add_fusion.place
  13.5 0.0 copy-done.4
  13.5 0.0 copy-done.3
  13.5 6.8 %shard_map.46 = (bf16[4,512,512]{2,1,0:T(8,128)(2,1)S(1)}, bf16[4,512,512]{2,1,0:T(8,128)(2,1)}, bf16[4,512,512]{2,1,0:T(8,128)(2,1)}, bf16[4,512,512]{2,1,0:T(8,128)(2,1)}) custom-call(s32[3]{0:T(128)S(1)} %pad_add_fusion.place, s32[8]{0:T(128)S(1)} %copy-done.4, s32[4,8,8]{2,1,0:T(8,128)S(1)} %copy-done.3, bf16[4,1024,1024]{2,1,0:T(8,128)(2,1)} %aux.1), custom_call_target="tpu_custom_call" | custom-call | bytes 16777216 | tf_op jit(solution)/shard_map/pallas_call | solution.py:69
  20.4 11.8 %all-to-all-done = bf16[64,8,1024]{2,1,0:T(8,128)(2,1)S(1)} async-done(((bf16[64,8,1024]{2,1,0:T(8,128)(2,1)}), bf16[64,8,1024]{2,1,0:T(8,128)(2,1)S(1)}, u32[]{:S(2)}, u32[]{:S(2)}) %all-to-all-start) | async-done | bytes 1048608 | tf_op jit(solution)/shard_map/all_to_all | solution.py:267
  32.2 0.0 copy-start
  32.2 0.0 copy-start.1
  32.2 0.0 copy-start.2
  32.2 0.0 collective-permute-start
  32.2 2.3 %shard_map.47.part = f32[512,4096]{1,0:T(8,128)S(1)} custom-call(bf16[4,512,512]{2,1,0:T(8,128)(2,1)S(1)} %get-tuple-element.20.send_own, bf16[512,1024]{1,0:T(8,128)(2,1)S(1)} %bitcast.11), custom_call_target="tpu_custom_call" | custom-call | flops 2147483648 | tf_op jit(solution)/shard_map/pallas_call | solution.py:95
  34.5 0.3 collective-permute-done.theirs
  34.8 0.0 copy-done
  34.8 0.0 copy-done.1
  34.8 0.2 copy-done.2
  35.0 3.5 %shard_map.50 = f32[2,1024,128]{2,1,0:T(8,128)S(1)} custom-call(bf16[4,512,512]{2,1,0:T(8,128)(2,1)S(1)} %get-tuple-element.20.send_own, bf16[4,512,512]{2,1,0:T(8,128)(2,1)S(1)} %copy-done, bf16[4,512,512]{2,1,0:T(8,128)(2,1)S(1)} %copy-done.1, bf16[4,512,512]{2,1,0:T(8,128)(2,1)S(1)} %copy-done.2, bf16[512,1024]{1,0:T(8,128)(2,1)S(1)} %collective-permute-done.theirs, ...), custom_call_target="tpu_custom_call" | custom-call | flops 3221225472 | tf_op jit(solution)/shard_map/pallas_call | solution.py:136
  38.5 0.1 collective-permute-start.2
  38.6 3.5 %shard_map.48 = f32[2,1024,128]{2,1,0:T(8,128)S(1)} custom-call(bf16[4,512,512]{2,1,0:T(8,128)(2,1)S(1)} %get-tuple-element.20.send_own, bf16[4,512,512]{2,1,0:T(8,128)(2,1)S(1)} %copy-done, bf16[4,512,512]{2,1,0:T(8,128)(2,1)S(1)} %copy-done.1, bf16[4,512,512]{2,1,0:T(8,128)(2,1)S(1)} %copy-done.2, bf16[512,1024]{1,0:T(8,128)(2,1)S(1)} %collective-permute-done.theirs, ...), custom_call_target="tpu_custom_call" | custom-call | flops 3221225472 | tf_op jit(solution)/shard_map/pallas_call | solution.py:136
  42.1 0.7 collective-permute-start.1
  42.8 0.0 collective-permute-done.2.got
  42.9 5.2 %shard_map.51 = (bf16[1024,128]{1,0:T(8,128)(2,1)S(1)}, bf16[1024,128]{1,0:T(8,128)(2,1)S(1)}) custom-call(s32[3]{0:T(128)S(1)} %pad_add_fusion.place, bf16[4,512,512]{2,1,0:T(8,128)(2,1)S(1)} %get-tuple-element.20.send_own, bf16[4,512,512]{2,1,0:T(8,128)(2,1)S(1)} %copy-done, bf16[4,512,512]{2,1,0:T(8,128)(2,1)S(1)} %copy-done.1, ...), custom_call_target="tpu_custom_call" | custom-call | flops 4294967296 | tf_op jit(solution)/shard_map/pallas_call | solution.py:179
  48.1 0.4 collective-permute-start.3
  48.4 3.0 %collective-permute-start.4 = (bf16[1024,128]{1,0:T(8,128)(2,1)S(1)}, bf16[1024,128]{1,0:T(8,128)(2,1)S(1)}, u32[]{:S(2)}, u32[]{:S(2)}) collective-permute-start(bf16[1024,128]{1,0:T(8,128)(2,1)S(1)} %get-tuple-element.26), channel_id=1, source_target_pairs={{0,96},{32,0},{64,32},{96,64},{1,97},{33,1},{65,33},{97,65},{2,98}... | collective-permute-start | bytes 786440 | tf_op jit(solution)/shard_map/ppermute | solution.py:274
  51.4 0.0 collective-permute-done.1.got
  51.4 4.6 %shard_map.49.far = f32[2,1024,128]{2,1,0:T(8,128)S(1)} custom-call(bf16[4,512,512]{2,1,0:T(8,128)(2,1)S(1)} %get-tuple-element.20.send_own, bf16[4,512,512]{2,1,0:T(8,128)(2,1)S(1)} %copy-done, bf16[4,512,512]{2,1,0:T(8,128)(2,1)S(1)} %copy-done.1, bf16[4,512,512]{2,1,0:T(8,128)(2,1)S(1)} %copy-done.2, bf16[512,1024]{1,0:T(8,128)(2,1)S(1)} %bitcast.13, ...), custom_call_target="tpu_custom_call" | custom-call | flops 4294967296 | tf_op jit(solution)/shard_map/pallas_call | solution.py:200
  55.9 1.7 %collective-permute-done.3.low = bf16[1024,128]{1,0:T(8,128)(2,1)S(1)} collective-permute-done((bf16[1024,128]{1,0:T(8,128)(2,1)S(1)}, bf16[1024,128]{1,0:T(8,128)(2,1)S(1)}, u32[]{:S(2)}, u32[]{:S(2)}) %collective-permute-start.3) | collective-permute-done | bytes 262176 | tf_op jit(solution)/shard_map/ppermute | solution.py:273
  57.6 0.0 collective-permute-done.4.high
  57.6 0.7 shard_map.52
  58.3 16.8 %all_to_all.10.parts = bf16[32,64,128]{2,1,0:T(8,128)(2,1)S(1)} all-to-all(bf16[32,64,128]{2,1,0:T(8,128)(2,1)S(1)} %bitcast.14), channel_id=1, replica_groups={{6,7,14,15,2,3,10,11,4,5,12,13,0,1,8,9,70,71,78,79,66,67,74,75,68,69,76..., dimensions={0} | all-to-all | bytes 1048576 | tf_op jit(solution)/shard_map/all_to_all | solution.py:279
  75.1 0.7 shard_map.53
  (1 shorter events, 0.0 us)
Async XLA Ops:
  0.0 13.5 %copy-start.4 = (s32[8]{0:T(128)S(1)}, s32[8]{0:T(128)}, u32[]{:S(2)}) copy-start(s32[8]{0:T(128)} %sizes.1) | copy-start | bytes 100
  0.0 13.5 %copy-start.3 = (s32[4,8,8]{2,1,0:T(8,128)S(1)}, s32[4,8,8]{2,1,0:T(8,128)}, u32[]{:S(2)}) copy-start(s32[4,8,8]{2,1,0:T(8,128)} %pattern.1) | copy-start | bytes 3076
  1.9 30.2 %all-to-all-start = ((bf16[64,8,1024]{2,1,0:T(8,128)(2,1)}), bf16[64,8,1024]{2,1,0:T(8,128)(2,1)S(1)}, u32[]{:S(2)}, u32[]{:S(2)}) async-start(bf16[64,8,1024]{2,1,0:T(8,128)(2,1)} %broadcast_in_dim.8), calls=%async_computation | async-start | bytes 2097152 | tf_op jit(solution)/shard_map/all_to_all | solution.py:267
  32.2 2.7 %copy-start = (bf16[4,512,512]{2,1,0:T(8,128)(2,1)S(1)}, bf16[4,512,512]{2,1,0:T(8,128)(2,1)}, u32[]{:S(2)}) copy-start(bf16[4,512,512]{2,1,0:T(8,128)(2,1)} %get-tuple-element.21.send_other) | copy-start | bytes 6291460
  32.2 2.7 %copy-start.1 = (bf16[4,512,512]{2,1,0:T(8,128)(2,1)S(1)}, bf16[4,512,512]{2,1,0:T(8,128)(2,1)}, u32[]{:S(2)}) copy-start(bf16[4,512,512]{2,1,0:T(8,128)(2,1)} %get-tuple-element.22.keep_own) | copy-start | bytes 6291460
  32.2 2.9 %copy-start.2 = (bf16[4,512,512]{2,1,0:T(8,128)(2,1)S(1)}, bf16[4,512,512]{2,1,0:T(8,128)(2,1)}, u32[]{:S(2)}) copy-start(bf16[4,512,512]{2,1,0:T(8,128)(2,1)} %get-tuple-element.23.keep_other) | copy-start | bytes 6291460
  32.2 2.7 %collective-permute-start = (bf16[512,1024]{1,0:T(8,128)(2,1)S(1)}, bf16[512,1024]{1,0:T(8,128)(2,1)S(1)}, u32[]{:S(2)}, u32[]{:S(2)}) collective-permute-start(bf16[512,1024]{1,0:T(8,128)(2,1)S(1)} %bitcast.10), channel_id=1, source_target_pairs={{0,16},{16,0},{1,17},{17,1},{2,18},{18,2},{3,19},{19,3},{4,20},{20... | collective-permute-start | bytes 3145736 | tf_op jit(solution)/shard_map/ppermute | solution.py:262
  38.5 4.3 %collective-permute-start.2 = (f32[2,1024,128]{2,1,0:T(8,128)S(1)}, f32[2,1024,128]{2,1,0:T(8,128)S(1)}, u32[]{:S(2)}, u32[]{:S(2)}) collective-permute-start(f32[2,1024,128]{2,1,0:T(8,128)S(1)} %shard_map.50), channel_id=1, source_target_pairs={{0,16},{16,0},{1,17},{17,1},{2,18},{18,2},{3,19},{19,3},{4,20},{20... | collective-permute-start | bytes 3145736 | tf_op jit(solution)/shard_map/ppermute | solution.py:262
  42.1 9.2 %collective-permute-start.1 = (f32[2,1024,128]{2,1,0:T(8,128)S(1)}, f32[2,1024,128]{2,1,0:T(8,128)S(1)}, u32[]{:S(2)}, u32[]{:S(2)}) collective-permute-start(f32[2,1024,128]{2,1,0:T(8,128)S(1)} %shard_map.48), channel_id=1, source_target_pairs={{0,16},{16,0},{1,17},{17,1},{2,18},{18,2},{3,19},{19,3},{4,20},{20... | collective-permute-start | bytes 3145736 | tf_op jit(solution)/shard_map/ppermute | solution.py:262
  48.1 9.5 %collective-permute-start.3 = (bf16[1024,128]{1,0:T(8,128)(2,1)S(1)}, bf16[1024,128]{1,0:T(8,128)(2,1)S(1)}, u32[]{:S(2)}, u32[]{:S(2)}) collective-permute-start(bf16[1024,128]{1,0:T(8,128)(2,1)S(1)} %get-tuple-element.25), channel_id=1, source_target_pairs={{0,32},{32,64},{64,96},{96,0},{1,33},{33,65},{65,97},{97,1},{2,34}... | collective-permute-start | bytes 786440 | tf_op jit(solution)/shard_map/ppermute | solution.py:273
  48.4 9.2 %collective-permute-start.4 = (bf16[1024,128]{1,0:T(8,128)(2,1)S(1)}, bf16[1024,128]{1,0:T(8,128)(2,1)S(1)}, u32[]{:S(2)}, u32[]{:S(2)}) collective-permute-start(bf16[1024,128]{1,0:T(8,128)(2,1)S(1)} %get-tuple-element.26), channel_id=1, source_target_pairs={{0,96},{32,0},{64,32},{96,64},{1,97},{33,1},{65,33},{97,65},{2,98}... | collective-permute-start | bytes 786440 | tf_op jit(solution)/shard_map/ppermute | solution.py:274

commit v6 on v5

--- a/solution.py
+++ b/solution.py
@@ -156,9 +156,10 @@
     return jnp.concatenate([got[h, HALF:, :], got[h, :HALF, :]], axis=0)
 
 
-def near_kernel(place, send_own, send_other, keep_own, keep_other, mine, theirs, got, up, down, coeff):
+def near_kernel(send_own, send_other, keep_own, keep_other, mine, theirs, got, up, down, coeff):
     keep_coeff(False, keep_own, keep_other, mine, theirs, coeff)
-    first_up = (place[2] == 0) | (place[2] == 3)
+    z = lax.axis_index("z")
+    first_up = (z == 0) | (z == 3)
 
     def store(h, value):
         value = (value + other_order(got, h)).astype(BF16)
@@ -175,16 +176,16 @@
     part_sums((send_own, send_other, keep_own, keep_other), coeff, store)
 
 
-def near_sums(place, aux, mine, theirs, got):
+def near_sums(aux, mine, theirs, got):
     return pl.pallas_call(
         near_kernel,
-        in_specs=[SMEM] + [VMEM] * 7,
+        in_specs=[VMEM] * 7,
         out_specs=[VMEM, VMEM],
         out_shape=[jax.ShapeDtypeStruct((N, BS), BF16)] * 2,
         scratch_shapes=[pltpu.VMEM((TILE, WIDE), BF16)],
         compiler_params=params(20),
         cost_estimate=cost(1),
-    )(place, *aux, mine, theirs, got)
+    )(*aux, mine, theirs, got)
 
 
 def far_kernel(send_own, send_other, keep_own, keep_other, mine, theirs, got, out, coeff):
@@ -208,23 +209,24 @@
     )(*aux, mine, theirs, got)
 
 
-def join_kernel(place, far, low, high, out):
+def join_kernel(far, low, high, out):
+    own_slot = lax.axis_index("z") // 2
     for i, j in enumerate((1, 0, 3, 2)):
         to, at = slice(i * TILE, (i + 1) * TILE), slice(j * TILE, (j + 1) * TILE)
         both = low[at, :].astype(F32) + high[at, :].astype(F32)
         for h in range(TILE // BS):
-            own = (place[2] // 2 == h).astype(F32)
+            own = (own_slot == h).astype(F32)
             out[h, to, :] = (far[h, to, :] + both * own).astype(BF16)
 
 
-def join(place, far, low, high):
+def join(far, low, high):
     return pl.pallas_call(
         join_kernel,
-        in_specs=[SMEM, VMEM, VMEM, VMEM],
+        in_specs=[VMEM, VMEM, VMEM],
         out_specs=VMEM,
         out_shape=jax.ShapeDtypeStruct((TILE // BS, N, BS), BF16),
         compiler_params=params(20),
-    )(place, far, low, high)
+    )(far, low, high)
 
 
 def finish_kernel(parts, out):
@@ -255,8 +257,7 @@
 
 def local(aux_ints, density, pattern, block_sizes):
     core = lax.axis_index("c")
-    z = lax.axis_index("z")
-    place = jnp.stack([core, lax.rem(z, 2), z])
+    place = jnp.stack([core, lax.rem(lax.axis_index("z"), 2)])
 
     def swap(array):
         return lax.ppermute(array, "c", [(0, 1), (1, 0)])
@@ -269,12 +270,12 @@
     theirs = swap(mine)
     part = first_part(aux[0], mine)
     got = swap(send_sums(False, aux, theirs, part))
-    up, down = near_sums(place, aux, mine, theirs, got)
+    up, down = near_sums(aux, mine, theirs, got)
     low = lax.ppermute(up, "z", [(i, (i + 1) % 4) for i in range(4)])
     high = lax.ppermute(down, "z", [(i, (i - 1) % 4) for i in range(4)])
     got = swap(send_sums(True, aux, theirs, part))
     far = far_sums(aux, mine, theirs, got)
-    chip = join(place, far, low, high)
+    chip = join(far, low, high)
     chip = chip.reshape(CHIP_COUNT // 2, BS // 2, BS)
     parts = lax.all_to_all(chip, ("z", "c", "x", "y"), 0, 0, axis_index_groups=sums_groups())
     return finish(parts).T

time: 76.3 us -> 75 us (0.983)
  Pallas kernels: 27.3 us -> 26 us
    pallas_call x2, Pallas kernels: 5.89 us -> 4.74 us  [the longest x1 4.6 us: near_sums(): pl.pallas_call(near_kernel, in_specs=[VMEM] * 7, out_specs=[VMEM, VMEM],...]
  transfers between devices with their start and end apart: 6 -> 6, of which waited for: 3 -> 3; matrix products, arithmetic and copies ran while one was open for 0% -> 0% of each run, Pallas kernels for 30% -> 29%
where the time goes in v6:
time: 75 us; the launch traced here: 74.6 us
  Pallas kernels  26 us (35%)
  blocking collectives  16.8 us (22%)
  starting transfers between devices  15.7 us (21%)
  waiting for transfers between devices  13.8 us (18%)
  local copies, waits for them, and re-layouts  1.33 us (2%)
  other arithmetic  0.88 us (1%)
    all_to_all x1, blocking collectives, local(): lax.all_to_all(chip, ('z', 'c', 'x', 'y'), 0, 0, axis_index_groups=sums_g...  16.8 us
    all_to_all x1, waiting for transfers between devices, local(): mine = lax.all_to_all(everyone, CHIPS, 0, 0).reshape(HALF, N)  11.8 us
    all_to_all x1, starting transfers between devices, local(): mine = lax.all_to_all(everyone, CHIPS, 0, 0).reshape(HALF, N)  11.5 us
    pallas_call x1, Pallas kernels, prepare(): pl.pallas_call(prepare_kernel, grid=(P_DEV,), in_specs=[SMEM, SMEM, SMEM,...  6.84 us
    pallas_call x2, Pallas kernels, send_sums(): pl.pallas_call(functools.partial(send_kernel, far), in_specs=[VMEM] * 6,...  6.83 us
    pallas_call x1, Pallas kernels, near_sums(): pl.pallas_call(near_kernel, in_specs=[VMEM] * 7, out_specs=[VMEM, VMEM],...  4.6 us
    pallas_call x1, Pallas kernels, far_sums(): pl.pallas_call(far_kernel, in_specs=[VMEM] * 7, out_specs=VMEM, out_shape...  4.49 us
    ppermute x1, starting transfers between devices, local(): high = lax.ppermute(down, 'z', [(i, (i - 1) % 4) for i in range(4)])  2.94 us
  transfers between devices with their start and end apart: 6, of which 3 were waited for; matrix products, arithmetic and copies ran while one was open for 0% of the time, Pallas kernels for 29%

profile of v6, /device:TPU:0, one launch (start us, length us, event | category | flops | bytes accessed | tf_op | source)
XLA Modules:
  0.0 74.6 jit_solution(17053020707233754751)
XLA Ops:
  0.0 0.0 copy-start.4
  0.0 0.0 copy-start.3
  0.0 0.8 %reverse_select_fusion = bf16[8,2,4,128]{3,0,1,2:T(8,128)(2,1)S(1)} fusion(bf16[8,2,4,128]{3,0,1,2:T(8,128)(2,1)} %bitcast.15, pred[]{:T(512)S(6)} %eq.3), kind=kLoop, calls=%fused_computation | loop fusion | flops 8192 | bytes 32769 | tf_op jit(solution)/shard_map/jit(_where)/select_n | solution.py:266
  0.8 1.1 %broadcast_in_dim.8 = bf16[64,8,1024]{2,1,0:T(8,128)(2,1)} broadcast(bf16[8,1024]{1,0:T(8,128)(2,1)S(1)} %bitcast.14), dimensions={1,2} | broadcast | bytes 1064960 | tf_op jit(solution)/shard_map/broadcast_in_dim | solution.py:267
  1.9 11.5 %all-to-all-start = ((bf16[64,8,1024]{2,1,0:T(8,128)(2,1)}), bf16[64,8,1024]{2,1,0:T(8,128)(2,1)S(1)}, u32[]{:S(2)}, u32[]{:S(2)}) async-start(bf16[64,8,1024]{2,1,0:T(8,128)(2,1)} %broadcast_in_dim.8), calls=%async_computation | async-start | bytes 2097152 | tf_op jit(solution)/shard_map/all_to_all | solution.py:268
  13.4 0.1 pad_add_fusion.place
  13.5 0.0 copy-done.4
  13.5 0.0 copy-done.3
  13.5 6.8 %shard_map.46 = (bf16[4,512,512]{2,1,0:T(8,128)(2,1)S(1)}, bf16[4,512,512]{2,1,0:T(8,128)(2,1)}, bf16[4,512,512]{2,1,0:T(8,128)(2,1)}, bf16[4,512,512]{2,1,0:T(8,128)(2,1)}) custom-call(s32[2]{0:T(128)S(1)} %pad_add_fusion.place, s32[8]{0:T(128)S(1)} %copy-done.4, s32[4,8,8]{2,1,0:T(8,128)S(1)} %copy-done.3, bf16[4,1024,1024]{2,1,0:T(8,128)(2,1)} %aux.1), custom_call_target="tpu_custom_call" | custom-call | bytes 16777216 | tf_op jit(solution)/shard_map/pallas_call | solution.py:69
  20.4 11.8 %all-to-all-done = bf16[64,8,1024]{2,1,0:T(8,128)(2,1)S(1)} async-done(((bf16[64,8,1024]{2,1,0:T(8,128)(2,1)}), bf16[64,8,1024]{2,1,0:T(8,128)(2,1)S(1)}, u32[]{:S(2)}, u32[]{:S(2)}) %all-to-all-start) | async-done | bytes 1048608 | tf_op jit(solution)/shard_map/all_to_all | solution.py:268
  32.2 0.0 copy-start
  32.2 0.0 copy-start.1
  32.2 0.0 copy-start.2
  32.2 0.0 collective-permute-start
  32.2 2.3 %shard_map.47.part = f32[512,4096]{1,0:T(8,128)S(1)} custom-call(bf16[4,512,512]{2,1,0:T(8,128)(2,1)S(1)} %get-tuple-element.20.send_own, bf16[512,1024]{1,0:T(8,128)(2,1)S(1)} %bitcast.10), custom_call_target="tpu_custom_call" | custom-call | flops 2147483648 | tf_op jit(solution)/shard_map/pallas_call | solution.py:95
  34.5 0.3 collective-permute-done.theirs
  34.8 0.0 copy-done
  34.8 0.0 copy-done.1
  34.8 0.2 copy-done.2
  35.0 3.4 %shard_map.50 = f32[2,1024,128]{2,1,0:T(8,128)S(1)} custom-call(bf16[4,512,512]{2,1,0:T(8,128)(2,1)S(1)} %get-tuple-element.20.send_own, bf16[4,512,512]{2,1,0:T(8,128)(2,1)S(1)} %copy-done, bf16[4,512,512]{2,1,0:T(8,128)(2,1)S(1)} %copy-done.1, bf16[4,512,512]{2,1,0:T(8,128)(2,1)S(1)} %copy-done.2, bf16[512,1024]{1,0:T(8,128)(2,1)S(1)} %collective-permute-done.theirs, ...), custom_call_target="tpu_custom_call" | custom-call | flops 3221225472 | tf_op jit(solution)/shard_map/pallas_call | solution.py:136
  38.4 0.1 collective-permute-start.2
  38.6 3.4 %shard_map.48 = f32[2,1024,128]{2,1,0:T(8,128)S(1)} custom-call(bf16[4,512,512]{2,1,0:T(8,128)(2,1)S(1)} %get-tuple-element.20.send_own, bf16[4,512,512]{2,1,0:T(8,128)(2,1)S(1)} %copy-done, bf16[4,512,512]{2,1,0:T(8,128)(2,1)S(1)} %copy-done.1, bf16[4,512,512]{2,1,0:T(8,128)(2,1)S(1)} %copy-done.2, bf16[512,1024]{1,0:T(8,128)(2,1)S(1)} %collective-permute-done.theirs, ...), custom_call_target="tpu_custom_call" | custom-call | flops 3221225472 | tf_op jit(solution)/shard_map/pallas_call | solution.py:136
  42.0 0.7 collective-permute-start.1
  42.7 0.0 collective-permute-done.2.got
  42.7 4.6 %shard_map.51 = (bf16[1024,128]{1,0:T(8,128)(2,1)S(1)}, bf16[1024,128]{1,0:T(8,128)(2,1)S(1)}) custom-call(bf16[4,512,512]{2,1,0:T(8,128)(2,1)S(1)} %get-tuple-element.20.send_own, bf16[4,512,512]{2,1,0:T(8,128)(2,1)S(1)} %copy-done, bf16[4,512,512]{2,1,0:T(8,128)(2,1)S(1)} %copy-done.1, bf16[4,512,512]{2,1,0:T(8,128)(2,1)S(1)} %copy-done.2, ...), custom_call_target="tpu_custom_call" | custom-call | flops 4294967296 | tf_op jit(solution)/shard_map/pallas_call | solution.py:180
  47.3 0.4 collective-permute-start.3
  47.7 2.9 %collective-permute-start.4 = (bf16[1024,128]{1,0:T(8,128)(2,1)S(1)}, bf16[1024,128]{1,0:T(8,128)(2,1)S(1)}, u32[]{:S(2)}, u32[]{:S(2)}) collective-permute-start(bf16[1024,128]{1,0:T(8,128)(2,1)S(1)} %get-tuple-element.26), channel_id=1, source_target_pairs={{0,96},{32,0},{64,32},{96,64},{1,97},{33,1},{65,33},{97,65},{2,98}... | collective-permute-start | bytes 786440 | tf_op jit(solution)/shard_map/ppermute | solution.py:275
  50.6 0.0 collective-permute-done.1.got
  50.6 4.5 %shard_map.49.far = f32[2,1024,128]{2,1,0:T(8,128)S(1)} custom-call(bf16[4,512,512]{2,1,0:T(8,128)(2,1)S(1)} %get-tuple-element.20.send_own, bf16[4,512,512]{2,1,0:T(8,128)(2,1)S(1)} %copy-done, bf16[4,512,512]{2,1,0:T(8,128)(2,1)S(1)} %copy-done.1, bf16[4,512,512]{2,1,0:T(8,128)(2,1)S(1)} %copy-done.2, bf16[512,1024]{1,0:T(8,128)(2,1)S(1)} %bitcast.12, ...), custom_call_target="tpu_custom_call" | custom-call | flops 4294967296 | tf_op jit(solution)/shard_map/pallas_call | solution.py:201
  55.1 1.7 %collective-permute-done.3.low = bf16[1024,128]{1,0:T(8,128)(2,1)S(1)} collective-permute-done((bf16[1024,128]{1,0:T(8,128)(2,1)S(1)}, bf16[1024,128]{1,0:T(8,128)(2,1)S(1)}, u32[]{:S(2)}, u32[]{:S(2)}) %collective-permute-start.3) | collective-permute-done | bytes 262176 | tf_op jit(solution)/shard_map/ppermute | solution.py:274
  56.9 0.0 collective-permute-done.4.high
  56.9 0.1 shard_map.52
  57.0 16.8 %all_to_all.10.parts = bf16[32,64,128]{2,1,0:T(8,128)(2,1)S(1)} all-to-all(bf16[32,64,128]{2,1,0:T(8,128)(2,1)S(1)} %bitcast.13), channel_id=1, replica_groups={{6,7,14,15,2,3,10,11,4,5,12,13,0,1,8,9,70,71,78,79,66,67,74,75,68,69,76..., dimensions={0} | all-to-all | bytes 1048576 | tf_op jit(solution)/shard_map/all_to_all | solution.py:280
  73.9 0.7 shard_map.53
  (1 shorter events, 0.0 us)
Async XLA Ops:
  0.0 13.5 %copy-start.4 = (s32[8]{0:T(128)S(1)}, s32[8]{0:T(128)}, u32[]{:S(2)}) copy-start(s32[8]{0:T(128)} %sizes.1) | copy-start | bytes 100
  0.0 13.5 %copy-start.3 = (s32[4,8,8]{2,1,0:T(8,128)S(1)}, s32[4,8,8]{2,1,0:T(8,128)}, u32[]{:S(2)}) copy-start(s32[4,8,8]{2,1,0:T(8,128)} %pattern.1) | copy-start | bytes 3076
  1.9 30.2 %all-to-all-start = ((bf16[64,8,1024]{2,1,0:T(8,128)(2,1)}), bf16[64,8,1024]{2,1,0:T(8,128)(2,1)S(1)}, u32[]{:S(2)}, u32[]{:S(2)}) async-start(bf16[64,8,1024]{2,1,0:T(8,128)(2,1)} %broadcast_in_dim.8), calls=%async_computation | async-start | bytes 2097152 | tf_op jit(solution)/shard_map/all_to_all | solution.py:268
  32.2 2.7 %copy-start = (bf16[4,512,512]{2,1,0:T(8,128)(2,1)S(1)}, bf16[4,512,512]{2,1,0:T(8,128)(2,1)}, u32[]{:S(2)}) copy-start(bf16[4,512,512]{2,1,0:T(8,128)(2,1)} %get-tuple-element.21.send_other) | copy-start | bytes 6291460
  32.2 2.7 %copy-start.1 = (bf16[4,512,512]{2,1,0:T(8,128)(2,1)S(1)}, bf16[4,512,512]{2,1,0:T(8,128)(2,1)}, u32[]{:S(2)}) copy-start(bf16[4,512,512]{2,1,0:T(8,128)(2,1)} %get-tuple-element.22.keep_own) | copy-start | bytes 6291460
  32.2 2.9 %copy-start.2 = (bf16[4,512,512]{2,1,0:T(8,128)(2,1)S(1)}, bf16[4,512,512]{2,1,0:T(8,128)(2,1)}, u32[]{:S(2)}) copy-start(bf16[4,512,512]{2,1,0:T(8,128)(2,1)} %get-tuple-element.23.keep_other) | copy-start | bytes 6291460
  32.2 2.7 %collective-permute-start = (bf16[512,1024]{1,0:T(8,128)(2,1)S(1)}, bf16[512,1024]{1,0:T(8,128)(2,1)S(1)}, u32[]{:S(2)}, u32[]{:S(2)}) collective-permute-start(bf16[512,1024]{1,0:T(8,128)(2,1)S(1)} %bitcast.9), channel_id=1, source_target_pairs={{0,16},{16,0},{1,17},{17,1},{2,18},{18,2},{3,19},{19,3},{4,20},{20... | collective-permute-start | bytes 3145736 | tf_op jit(solution)/shard_map/ppermute | solution.py:263
  38.4 4.3 %collective-permute-start.2 = (f32[2,1024,128]{2,1,0:T(8,128)S(1)}, f32[2,1024,128]{2,1,0:T(8,128)S(1)}, u32[]{:S(2)}, u32[]{:S(2)}) collective-permute-start(f32[2,1024,128]{2,1,0:T(8,128)S(1)} %shard_map.50), channel_id=1, source_target_pairs={{0,16},{16,0},{1,17},{17,1},{2,18},{18,2},{3,19},{19,3},{4,20},{20... | collective-permute-start | bytes 3145736 | tf_op jit(solution)/shard_map/ppermute | solution.py:263
  42.0 8.6 %collective-permute-start.1 = (f32[2,1024,128]{2,1,0:T(8,128)S(1)}, f32[2,1024,128]{2,1,0:T(8,128)S(1)}, u32[]{:S(2)}, u32[]{:S(2)}) collective-permute-start(f32[2,1024,128]{2,1,0:T(8,128)S(1)} %shard_map.48), channel_id=1, source_target_pairs={{0,16},{16,0},{1,17},{17,1},{2,18},{18,2},{3,19},{19,3},{4,20},{20... | collective-permute-start | bytes 3145736 | tf_op jit(solution)/shard_map/ppermute | solution.py:263
  47.3 9.5 %collective-permute-start.3 = (bf16[1024,128]{1,0:T(8,128)(2,1)S(1)}, bf16[1024,128]{1,0:T(8,128)(2,1)S(1)}, u32[]{:S(2)}, u32[]{:S(2)}) collective-permute-start(bf16[1024,128]{1,0:T(8,128)(2,1)S(1)} %get-tuple-element.25), channel_id=1, source_target_pairs={{0,32},{32,64},{64,96},{96,0},{1,33},{33,65},{65,97},{97,1},{2,34}... | collective-permute-start | bytes 786440 | tf_op jit(solution)/shard_map/ppermute | solution.py:274
  47.7 9.2 %collective-permute-start.4 = (bf16[1024,128]{1,0:T(8,128)(2,1)S(1)}, bf16[1024,128]{1,0:T(8,128)(2,1)S(1)}, u32[]{:S(2)}, u32[]{:S(2)}) collective-permute-start(bf16[1024,128]{1,0:T(8,128)(2,1)S(1)} %get-tuple-element.26), channel_id=1, source_target_pairs={{0,96},{32,0},{64,32},{96,64},{1,97},{33,1},{65,33},{97,65},{2,98}... | collective-permute-start | bytes 786440 | tf_op jit(solution)/shard_map/ppermute | solution.py:275

commit v7 on v6

--- a/solution.py
+++ b/solution.py
@@ -18,6 +18,7 @@
 TILE = 256
 CHIP_COUNT = 64
 ROWS = 8
+SPREAD = 8
 NN = (((1,), (0,)), ((), ()))
 NT = (((1,), (1,)), ((), ()))
 CHIPS = ("z", "x", "y")
@@ -44,6 +45,29 @@
 
 def block(index):
     return pl.ds(pl.multiple_of(index * BS, BS), BS)
+
+
+def spread_kernel(dens, out, copies, sems):
+    order = core_order(lax.axis_index("c"))
+    rows = jnp.concatenate([dens[:, block(b)] for b in order], axis=1)
+    for i in range(SPREAD):
+        copies[i] = rows
+    sends = [pltpu.make_async_copy(copies, out.at[i * SPREAD:(i + 1) * SPREAD], sems.at[i]) for i in range(CHIP_COUNT // SPREAD)]
+    for send in sends:
+        send.start()
+    for send in sends:
+        send.wait()
+
+
+def spread(density):
+    return pl.pallas_call(
+        spread_kernel,
+        in_specs=[VMEM],
+        out_specs=pl.BlockSpec(memory_space=pltpu.HBM),
+        out_shape=pltpu.HBM((CHIP_COUNT, ROWS, N), BF16),
+        scratch_shapes=[pltpu.VMEM((SPREAD, ROWS, N), BF16), pltpu.SemaphoreType.DMA((CHIP_COUNT // SPREAD,))],
+        compiler_params=params(8),
+    )(density)
 
 
 def prepare_kernel(place, sizes, pattern, aux, send_own, send_other, keep_own, keep_other):
@@ -262,10 +286,7 @@
     def swap(array):
         return lax.ppermute(array, "c", [(0, 1), (1, 0)])
 
-    blocks = density.reshape(ROWS, NB // 2, 2, BS).swapaxes(1, 2)
-    blocks = jnp.where(core == 0, blocks, blocks[:, ::-1]).reshape(ROWS, N)
-    everyone = jnp.broadcast_to(blocks[None], (CHIP_COUNT, ROWS, N))
-    mine = lax.all_to_all(everyone, CHIPS, 0, 0).reshape(HALF, N)
+    mine = lax.all_to_all(spread(density), CHIPS, 0, 0).reshape(HALF, N)
     mine, aux = lax.optimization_barrier((mine, prepare(place, block_sizes, pattern, aux_ints)))
     theirs = swap(mine)
     part = first_part(aux[0], mine)

time: 75 us -> 74.9 us (level)
  Pallas kernels: 26 us -> 27.1 us
  other arithmetic: 0.88 us -> 0.08 us
    broadcast_in_dim x1 -> x0, local copies, waits for them, and re-layouts: 1.13 us -> none  [local(): everyone = jnp.broadcast_to(blocks[None], (CHIP_COUNT, ROWS, N))]
    pallas_call x0 -> x1, Pallas kernels: none -> 1.09 us  [spread(): pl.pallas_call(spread_kernel, in_specs=[VMEM], out_specs=pl.BlockSpec(mem...]
    select_n x1 -> x0, other arithmetic: 0.8 us -> none  [local(): blocks = jnp.where(core == 0, blocks, blocks[:, ::-1]).reshape(ROWS, N)]
where the time goes in v7:
time: 74.9 us; the launch traced here: 74.5 us
  Pallas kernels  27.1 us (36%)
  blocking collectives  16.8 us (22%)
  starting transfers between devices  15.7 us (21%)
  waiting for transfers between devices  13.8 us (18%)
  local copies, waits for them, and re-layouts  0.92 us (1%)
    all_to_all x1, blocking collectives, local(): lax.all_to_all(chip, ('z', 'c', 'x', 'y'), 0, 0, axis_index_groups=sums_g...  16.8 us
    all_to_all x1, waiting for transfers between devices, local(): mine = lax.all_to_all(spread(density), CHIPS, 0, 0).reshape(HALF, N)  11.8 us
    all_to_all x1, starting transfers between devices, local(): mine = lax.all_to_all(spread(density), CHIPS, 0, 0).reshape(HALF, N)  11.5 us
    pallas_call x1, Pallas kernels, prepare(): pl.pallas_call(prepare_kernel, grid=(P_DEV,), in_specs=[SMEM, SMEM, SMEM,...  6.85 us
    pallas_call x2, Pallas kernels, send_sums(): pl.pallas_call(functools.partial(send_kernel, far), in_specs=[VMEM] * 6,...  6.83 us
    pallas_call x1, Pallas kernels, near_sums(): pl.pallas_call(near_kernel, in_specs=[VMEM] * 7, out_specs=[VMEM, VMEM],...  4.6 us
    pallas_call x1, Pallas kernels, far_sums(): pl.pallas_call(far_kernel, in_specs=[VMEM] * 7, out_specs=VMEM, out_shape...  4.49 us
    ppermute x1, starting transfers between devices, local(): high = lax.ppermute(down, 'z', [(i, (i - 1) % 4) for i in range(4)])  2.94 us
  transfers between devices with their start and end apart: 6, of which 3 were waited for; matrix products, arithmetic and copies ran while one was open for 0% of the time, Pallas kernels for 29%

profile of v7, /device:TPU:0, one launch (start us, length us, event | category | flops | bytes accessed | tf_op | source)
XLA Modules:
  0.0 74.5 jit_solution(4150762410275118251)
XLA Ops:
  0.0 0.0 copy-start.3
  0.0 0.7 copy-done.3
  0.7 0.0 copy-start.4
  0.7 0.0 copy-start.5
  0.7 1.1 %shard_map.46 = bf16[64,8,1024]{2,1,0:T(8,128)(2,1)} custom-call(bf16[8,1024]{1,0:T(8,128)(2,1)S(1)} %copy-done.3), custom_call_target="tpu_custom_call" | custom-call | tf_op jit(solution)/shard_map/pallas_call | solution.py:63
  1.8 11.5 %all-to-all-start = ((bf16[64,8,1024]{2,1,0:T(8,128)(2,1)}), bf16[64,8,1024]{2,1,0:T(8,128)(2,1)S(1)}, u32[]{:S(2)}, u32[]{:S(2)}) async-start(bf16[64,8,1024]{2,1,0:T(8,128)(2,1)} %shard_map.46), calls=%async_computation | async-start | bytes 2097152 | tf_op jit(solution)/shard_map/all_to_all | solution.py:289
  13.3 0.1 pad_add_fusion.place
  13.4 0.0 copy-done.4
  13.4 0.0 copy-done.5
  13.4 6.9 %shard_map.47 = (bf16[4,512,512]{2,1,0:T(8,128)(2,1)S(1)}, bf16[4,512,512]{2,1,0:T(8,128)(2,1)}, bf16[4,512,512]{2,1,0:T(8,128)(2,1)}, bf16[4,512,512]{2,1,0:T(8,128)(2,1)}) custom-call(s32[2]{0:T(128)S(1)} %pad_add_fusion.place, s32[8]{0:T(128)S(1)} %copy-done.5, s32[4,8,8]{2,1,0:T(8,128)S(1)} %copy-done.4, bf16[4,1024,1024]{2,1,0:T(8,128)(2,1)} %aux.1), custom_call_target="tpu_custom_call" | custom-call | bytes 16777216 | tf_op jit(solution)/shard_map/pallas_call | solution.py:93
  20.3 11.8 %all-to-all-done = bf16[64,8,1024]{2,1,0:T(8,128)(2,1)S(1)} async-done(((bf16[64,8,1024]{2,1,0:T(8,128)(2,1)}), bf16[64,8,1024]{2,1,0:T(8,128)(2,1)S(1)}, u32[]{:S(2)}, u32[]{:S(2)}) %all-to-all-start) | async-done | bytes 1048608 | tf_op jit(solution)/shard_map/all_to_all | solution.py:289
  32.1 0.0 copy-start
  32.1 0.0 copy-start.1
  32.1 0.0 copy-start.2
  32.1 0.0 collective-permute-start
  32.1 2.3 %shard_map.48.part = f32[512,4096]{1,0:T(8,128)S(1)} custom-call(bf16[4,512,512]{2,1,0:T(8,128)(2,1)S(1)} %get-tuple-element.20.send_own, bf16[512,1024]{1,0:T(8,128)(2,1)S(1)} %bitcast.6), custom_call_target="tpu_custom_call" | custom-call | flops 2147483648 | tf_op jit(solution)/shard_map/pallas_call | solution.py:119
  34.4 0.3 collective-permute-done.theirs
  34.7 0.0 copy-done
  34.7 0.0 copy-done.1
  34.7 0.2 copy-done.2
  34.9 3.4 %shard_map.51 = f32[2,1024,128]{2,1,0:T(8,128)S(1)} custom-call(bf16[4,512,512]{2,1,0:T(8,128)(2,1)S(1)} %get-tuple-element.20.send_own, bf16[4,512,512]{2,1,0:T(8,128)(2,1)S(1)} %copy-done, bf16[4,512,512]{2,1,0:T(8,128)(2,1)S(1)} %copy-done.1, bf16[4,512,512]{2,1,0:T(8,128)(2,1)S(1)} %copy-done.2, bf16[512,1024]{1,0:T(8,128)(2,1)S(1)} %collective-permute-done.theirs, ...), custom_call_target="tpu_custom_call" | custom-call | flops 3221225472 | tf_op jit(solution)/shard_map/pallas_call | solution.py:160
  38.3 0.1 collective-permute-start.2
  38.5 3.4 %shard_map.49 = f32[2,1024,128]{2,1,0:T(8,128)S(1)} custom-call(bf16[4,512,512]{2,1,0:T(8,128)(2,1)S(1)} %get-tuple-element.20.send_own, bf16[4,512,512]{2,1,0:T(8,128)(2,1)S(1)} %copy-done, bf16[4,512,512]{2,1,0:T(8,128)(2,1)S(1)} %copy-done.1, bf16[4,512,512]{2,1,0:T(8,128)(2,1)S(1)} %copy-done.2, bf16[512,1024]{1,0:T(8,128)(2,1)S(1)} %collective-permute-done.theirs, ...), custom_call_target="tpu_custom_call" | custom-call | flops 3221225472 | tf_op jit(solution)/shard_map/pallas_call | solution.py:160
  41.9 0.7 collective-permute-start.1
  42.6 0.0 collective-permute-done.2.got
  42.6 4.6 %shard_map.52 = (bf16[1024,128]{1,0:T(8,128)(2,1)S(1)}, bf16[1024,128]{1,0:T(8,128)(2,1)S(1)}) custom-call(bf16[4,512,512]{2,1,0:T(8,128)(2,1)S(1)} %get-tuple-element.20.send_own, bf16[4,512,512]{2,1,0:T(8,128)(2,1)S(1)} %copy-done, bf16[4,512,512]{2,1,0:T(8,128)(2,1)S(1)} %copy-done.1, bf16[4,512,512]{2,1,0:T(8,128)(2,1)S(1)} %copy-done.2, ...), custom_call_target="tpu_custom_call" | custom-call | flops 4294967296 | tf_op jit(solution)/shard_map/pallas_call | solution.py:204
  47.2 0.4 collective-permute-start.3
  47.6 2.9 %collective-permute-start.4 = (bf16[1024,128]{1,0:T(8,128)(2,1)S(1)}, bf16[1024,128]{1,0:T(8,128)(2,1)S(1)}, u32[]{:S(2)}, u32[]{:S(2)}) collective-permute-start(bf16[1024,128]{1,0:T(8,128)(2,1)S(1)} %get-tuple-element.26), channel_id=1, source_target_pairs={{0,96},{32,0},{64,32},{96,64},{1,97},{33,1},{65,33},{97,65},{2,98}... | collective-permute-start | bytes 786440 | tf_op jit(solution)/shard_map/ppermute | solution.py:296
  50.5 0.0 collective-permute-done.1.got
  50.5 4.5 %shard_map.50.far = f32[2,1024,128]{2,1,0:T(8,128)S(1)} custom-call(bf16[4,512,512]{2,1,0:T(8,128)(2,1)S(1)} %get-tuple-element.20.send_own, bf16[4,512,512]{2,1,0:T(8,128)(2,1)S(1)} %copy-done, bf16[4,512,512]{2,1,0:T(8,128)(2,1)S(1)} %copy-done.1, bf16[4,512,512]{2,1,0:T(8,128)(2,1)S(1)} %copy-done.2, bf16[512,1024]{1,0:T(8,128)(2,1)S(1)} %bitcast.8, ...), custom_call_target="tpu_custom_call" | custom-call | flops 4294967296 | tf_op jit(solution)/shard_map/pallas_call | solution.py:225
  55.0 1.7 %collective-permute-done.3.low = bf16[1024,128]{1,0:T(8,128)(2,1)S(1)} collective-permute-done((bf16[1024,128]{1,0:T(8,128)(2,1)S(1)}, bf16[1024,128]{1,0:T(8,128)(2,1)S(1)}, u32[]{:S(2)}, u32[]{:S(2)}) %collective-permute-start.3) | collective-permute-done | bytes 262176 | tf_op jit(solution)/shard_map/ppermute | solution.py:295
  56.8 0.0 collective-permute-done.4.high
  56.8 0.1 shard_map.53
  56.9 16.8 %all_to_all.10.parts = bf16[32,64,128]{2,1,0:T(8,128)(2,1)S(1)} all-to-all(bf16[32,64,128]{2,1,0:T(8,128)(2,1)S(1)} %bitcast.9), channel_id=1, replica_groups={{6,7,14,15,2,3,10,11,4,5,12,13,0,1,8,9,70,71,78,79,66,67,74,75,68,69,76..., dimensions={0} | all-to-all | bytes 1048576 | tf_op jit(solution)/shard_map/all_to_all | solution.py:301
  73.8 0.7 shard_map.54
Async XLA Ops:
  0.0 0.7 copy-start.3
  0.7 12.7 %copy-start.4 = (s32[4,8,8]{2,1,0:T(8,128)S(1)}, s32[4,8,8]{2,1,0:T(8,128)}, u32[]{:S(2)}) copy-start(s32[4,8,8]{2,1,0:T(8,128)} %pattern.1) | copy-start | bytes 3076
  0.7 12.7 %copy-start.5 = (s32[8]{0:T(128)S(1)}, s32[8]{0:T(128)}, u32[]{:S(2)}) copy-start(s32[8]{0:T(128)} %sizes.1) | copy-start | bytes 100
  1.8 30.2 %all-to-all-start = ((bf16[64,8,1024]{2,1,0:T(8,128)(2,1)}), bf16[64,8,1024]{2,1,0:T(8,128)(2,1)S(1)}, u32[]{:S(2)}, u32[]{:S(2)}) async-start(bf16[64,8,1024]{2,1,0:T(8,128)(2,1)} %shard_map.46), calls=%async_computation | async-start | bytes 2097152 | tf_op jit(solution)/shard_map/all_to_all | solution.py:289
  32.1 2.7 %copy-start = (bf16[4,512,512]{2,1,0:T(8,128)(2,1)S(1)}, bf16[4,512,512]{2,1,0:T(8,128)(2,1)}, u32[]{:S(2)}) copy-start(bf16[4,512,512]{2,1,0:T(8,128)(2,1)} %get-tuple-element.21.send_other) | copy-start | bytes 6291460
  32.1 2.7 %copy-start.1 = (bf16[4,512,512]{2,1,0:T(8,128)(2,1)S(1)}, bf16[4,512,512]{2,1,0:T(8,128)(2,1)}, u32[]{:S(2)}) copy-start(bf16[4,512,512]{2,1,0:T(8,128)(2,1)} %get-tuple-element.22.keep_own) | copy-start | bytes 6291460
  32.1 2.9 %copy-start.2 = (bf16[4,512,512]{2,1,0:T(8,128)(2,1)S(1)}, bf16[4,512,512]{2,1,0:T(8,128)(2,1)}, u32[]{:S(2)}) copy-start(bf16[4,512,512]{2,1,0:T(8,128)(2,1)} %get-tuple-element.23.keep_other) | copy-start | bytes 6291460
  32.1 2.7 %collective-permute-start = (bf16[512,1024]{1,0:T(8,128)(2,1)S(1)}, bf16[512,1024]{1,0:T(8,128)(2,1)S(1)}, u32[]{:S(2)}, u32[]{:S(2)}) collective-permute-start(bf16[512,1024]{1,0:T(8,128)(2,1)S(1)} %bitcast.5), channel_id=1, source_target_pairs={{0,16},{16,0},{1,17},{17,1},{2,18},{18,2},{3,19},{19,3},{4,20},{20... | collective-permute-start | bytes 3145736 | tf_op jit(solution)/shard_map/ppermute | solution.py:287
  38.3 4.3 %collective-permute-start.2 = (f32[2,1024,128]{2,1,0:T(8,128)S(1)}, f32[2,1024,128]{2,1,0:T(8,128)S(1)}, u32[]{:S(2)}, u32[]{:S(2)}) collective-permute-start(f32[2,1024,128]{2,1,0:T(8,128)S(1)} %shard_map.51), channel_id=1, source_target_pairs={{0,16},{16,0},{1,17},{17,1},{2,18},{18,2},{3,19},{19,3},{4,20},{20... | collective-permute-start | bytes 3145736 | tf_op jit(solution)/shard_map/ppermute | solution.py:287
  41.9 8.6 %collective-permute-start.1 = (f32[2,1024,128]{2,1,0:T(8,128)S(1)}, f32[2,1024,128]{2,1,0:T(8,128)S(1)}, u32[]{:S(2)}, u32[]{:S(2)}) collective-permute-start(f32[2,1024,128]{2,1,0:T(8,128)S(1)} %shard_map.49), channel_id=1, source_target_pairs={{0,16},{16,0},{1,17},{17,1},{2,18},{18,2},{3,19},{19,3},{4,20},{20... | collective-permute-start | bytes 3145736 | tf_op jit(solution)/shard_map/ppermute | solution.py:287
  47.2 9.5 %collective-permute-start.3 = (bf16[1024,128]{1,0:T(8,128)(2,1)S(1)}, bf16[1024,128]{1,0:T(8,128)(2,1)S(1)}, u32[]{:S(2)}, u32[]{:S(2)}) collective-permute-start(bf16[1024,128]{1,0:T(8,128)(2,1)S(1)} %get-tuple-element.25), channel_id=1, source_target_pairs={{0,32},{32,64},{64,96},{96,0},{1,33},{33,65},{65,97},{97,1},{2,34}... | collective-permute-start | bytes 786440 | tf_op jit(solution)/shard_map/ppermute | solution.py:295
  47.6 9.2 %collective-permute-start.4 = (bf16[1024,128]{1,0:T(8,128)(2,1)S(1)}, bf16[1024,128]{1,0:T(8,128)(2,1)S(1)}, u32[]{:S(2)}, u32[]{:S(2)}) collective-permute-start(bf16[1024,128]{1,0:T(8,128)(2,1)S(1)} %get-tuple-element.26), channel_id=1, source_target_pairs={{0,96},{32,0},{64,32},{96,64},{1,97},{33,1},{65,33},{97,65},{2,98}... | collective-permute-start | bytes 786440 | tf_op jit(solution)/shard_map/ppermute | solution.py:296

commit v8 on v6

--- a/solution.py
+++ b/solution.py
@@ -214,9 +214,8 @@
     for i, j in enumerate((1, 0, 3, 2)):
         to, at = slice(i * TILE, (i + 1) * TILE), slice(j * TILE, (j + 1) * TILE)
         both = low[at, :].astype(F32) + high[at, :].astype(F32)
-        for h in range(TILE // BS):
-            own = (own_slot == h).astype(F32)
-            out[h, to, :] = (far[h, to, :] + both * own).astype(BF16)
+        out[own_slot, to, :] = (far[own_slot, to, :] + both).astype(BF16)
+        out[1 - own_slot, to, :] = far[1 - own_slot, to, :].astype(BF16)
 
 
 def join(far, low, high):

time: 75 us -> 75 us (level)
  no operation moved by 1% of the time
where the time goes in v8:
time: 75 us; the launch traced here: 74.5 us
  Pallas kernels  25.9 us (35%)
  blocking collectives  16.8 us (22%)
  starting transfers between devices  15.7 us (21%)
  waiting for transfers between devices  13.8 us (18%)
  local copies, waits for them, and re-layouts  1.33 us (2%)
  other arithmetic  0.88 us (1%)
    all_to_all x1, blocking collectives, local(): lax.all_to_all(chip, ('z', 'c', 'x', 'y'), 0, 0, axis_index_groups=sums_g...  16.8 us
    all_to_all x1, waiting for transfers between devices, local(): mine = lax.all_to_all(everyone, CHIPS, 0, 0).reshape(HALF, N)  11.8 us
    all_to_all x1, starting transfers between devices, local(): mine = lax.all_to_all(everyone, CHIPS, 0, 0).reshape(HALF, N)  11.5 us
    pallas_call x1, Pallas kernels, prepare(): pl.pallas_call(prepare_kernel, grid=(P_DEV,), in_specs=[SMEM, SMEM, SMEM,...  6.84 us
    pallas_call x2, Pallas kernels, send_sums(): pl.pallas_call(functools.partial(send_kernel, far), in_specs=[VMEM] * 6,...  6.83 us
    pallas_call x1, Pallas kernels, near_sums(): pl.pallas_call(near_kernel, in_specs=[VMEM] * 7, out_specs=[VMEM, VMEM],...  4.6 us
    pallas_call x1, Pallas kernels, far_sums(): pl.pallas_call(far_kernel, in_specs=[VMEM] * 7, out_specs=VMEM, out_shape...  4.49 us
    ppermute x1, starting transfers between devices, local(): high = lax.ppermute(down, 'z', [(i, (i - 1) % 4) for i in range(4)])  2.94 us
  transfers between devices with their start and end apart: 6, of which 3 were waited for; matrix products, arithmetic and copies ran while one was open for 0% of the time, Pallas kernels for 29%

profile of v8, /device:TPU:0, one launch (start us, length us, event | category | flops | bytes accessed | tf_op | source)
XLA Modules:
  0.0 74.5 jit_solution(14981458992443782486)
XLA Ops:
  0.0 0.0 copy-start.4
  0.0 0.0 copy-start.3
  0.0 0.8 %reverse_select_fusion = bf16[8,2,4,128]{3,0,1,2:T(8,128)(2,1)S(1)} fusion(bf16[8,2,4,128]{3,0,1,2:T(8,128)(2,1)} %bitcast.15, pred[]{:T(512)S(6)} %eq.3), kind=kLoop, calls=%fused_computation | loop fusion | flops 8192 | bytes 32769 | tf_op jit(solution)/shard_map/jit(_where)/select_n | solution.py:265
  0.8 1.1 %broadcast_in_dim.8 = bf16[64,8,1024]{2,1,0:T(8,128)(2,1)} broadcast(bf16[8,1024]{1,0:T(8,128)(2,1)S(1)} %bitcast.14), dimensions={1,2} | broadcast | bytes 1064960 | tf_op jit(solution)/shard_map/broadcast_in_dim | solution.py:266
  1.9 11.5 %all-to-all-start = ((bf16[64,8,1024]{2,1,0:T(8,128)(2,1)}), bf16[64,8,1024]{2,1,0:T(8,128)(2,1)S(1)}, u32[]{:S(2)}, u32[]{:S(2)}) async-start(bf16[64,8,1024]{2,1,0:T(8,128)(2,1)} %broadcast_in_dim.8), calls=%async_computation | async-start | bytes 2097152 | tf_op jit(solution)/shard_map/all_to_all | solution.py:267
  13.4 0.1 pad_add_fusion.place
  13.5 0.0 copy-done.4
  13.5 0.0 copy-done.3
  13.5 6.8 %shard_map.46 = (bf16[4,512,512]{2,1,0:T(8,128)(2,1)S(1)}, bf16[4,512,512]{2,1,0:T(8,128)(2,1)}, bf16[4,512,512]{2,1,0:T(8,128)(2,1)}, bf16[4,512,512]{2,1,0:T(8,128)(2,1)}) custom-call(s32[2]{0:T(128)S(1)} %pad_add_fusion.place, s32[8]{0:T(128)S(1)} %copy-done.4, s32[4,8,8]{2,1,0:T(8,128)S(1)} %copy-done.3, bf16[4,1024,1024]{2,1,0:T(8,128)(2,1)} %aux.1), custom_call_target="tpu_custom_call" | custom-call | bytes 16777216 | tf_op jit(solution)/shard_map/pallas_call | solution.py:69
  20.4 11.8 %all-to-all-done = bf16[64,8,1024]{2,1,0:T(8,128)(2,1)S(1)} async-done(((bf16[64,8,1024]{2,1,0:T(8,128)(2,1)}), bf16[64,8,1024]{2,1,0:T(8,128)(2,1)S(1)}, u32[]{:S(2)}, u32[]{:S(2)}) %all-to-all-start) | async-done | bytes 1048608 | tf_op jit(solution)/shard_map/all_to_all | solution.py:267
  32.2 0.0 copy-start
  32.2 0.0 copy-start.1
  32.2 0.0 copy-start.2
  32.2 0.0 collective-permute-start
  32.2 2.3 %shard_map.47.part = f32[512,4096]{1,0:T(8,128)S(1)} custom-call(bf16[4,512,512]{2,1,0:T(8,128)(2,1)S(1)} %get-tuple-element.20.send_own, bf16[512,1024]{1,0:T(8,128)(2,1)S(1)} %bitcast.10), custom_call_target="tpu_custom_call" | custom-call | flops 2147483648 | tf_op jit(solution)/shard_map/pallas_call | solution.py:95
  34.5 0.3 collective-permute-done.theirs
  34.8 0.0 copy-done
  34.8 0.0 copy-done.1
  34.8 0.2 copy-done.2
  35.0 3.4 %shard_map.50 = f32[2,1024,128]{2,1,0:T(8,128)S(1)} custom-call(bf16[4,512,512]{2,1,0:T(8,128)(2,1)S(1)} %get-tuple-element.20.send_own, bf16[4,512,512]{2,1,0:T(8,128)(2,1)S(1)} %copy-done, bf16[4,512,512]{2,1,0:T(8,128)(2,1)S(1)} %copy-done.1, bf16[4,512,512]{2,1,0:T(8,128)(2,1)S(1)} %copy-done.2, bf16[512,1024]{1,0:T(8,128)(2,1)S(1)} %collective-permute-done.theirs, ...), custom_call_target="tpu_custom_call" | custom-call | flops 3221225472 | tf_op jit(solution)/shard_map/pallas_call | solution.py:136
  38.4 0.1 collective-permute-start.2
  38.6 3.4 %shard_map.48 = f32[2,1024,128]{2,1,0:T(8,128)S(1)} custom-call(bf16[4,512,512]{2,1,0:T(8,128)(2,1)S(1)} %get-tuple-element.20.send_own, bf16[4,512,512]{2,1,0:T(8,128)(2,1)S(1)} %copy-done, bf16[4,512,512]{2,1,0:T(8,128)(2,1)S(1)} %copy-done.1, bf16[4,512,512]{2,1,0:T(8,128)(2,1)S(1)} %copy-done.2, bf16[512,1024]{1,0:T(8,128)(2,1)S(1)} %collective-permute-done.theirs, ...), custom_call_target="tpu_custom_call" | custom-call | flops 3221225472 | tf_op jit(solution)/shard_map/pallas_call | solution.py:136
  42.0 0.7 collective-permute-start.1
  42.7 0.0 collective-permute-done.2.got
  42.7 4.6 %shard_map.51 = (bf16[1024,128]{1,0:T(8,128)(2,1)S(1)}, bf16[1024,128]{1,0:T(8,128)(2,1)S(1)}) custom-call(bf16[4,512,512]{2,1,0:T(8,128)(2,1)S(1)} %get-tuple-element.20.send_own, bf16[4,512,512]{2,1,0:T(8,128)(2,1)S(1)} %copy-done, bf16[4,512,512]{2,1,0:T(8,128)(2,1)S(1)} %copy-done.1, bf16[4,512,512]{2,1,0:T(8,128)(2,1)S(1)} %copy-done.2, ...), custom_call_target="tpu_custom_call" | custom-call | flops 4294967296 | tf_op jit(solution)/shard_map/pallas_call | solution.py:180
  47.3 0.4 collective-permute-start.3
  47.7 2.9 %collective-permute-start.4 = (bf16[1024,128]{1,0:T(8,128)(2,1)S(1)}, bf16[1024,128]{1,0:T(8,128)(2,1)S(1)}, u32[]{:S(2)}, u32[]{:S(2)}) collective-permute-start(bf16[1024,128]{1,0:T(8,128)(2,1)S(1)} %get-tuple-element.26), channel_id=1, source_target_pairs={{0,96},{32,0},{64,32},{96,64},{1,97},{33,1},{65,33},{97,65},{2,98}... | collective-permute-start | bytes 786440 | tf_op jit(solution)/shard_map/ppermute | solution.py:274
  50.6 0.0 collective-permute-done.1.got
  50.6 4.5 %shard_map.49.far = f32[2,1024,128]{2,1,0:T(8,128)S(1)} custom-call(bf16[4,512,512]{2,1,0:T(8,128)(2,1)S(1)} %get-tuple-element.20.send_own, bf16[4,512,512]{2,1,0:T(8,128)(2,1)S(1)} %copy-done, bf16[4,512,512]{2,1,0:T(8,128)(2,1)S(1)} %copy-done.1, bf16[4,512,512]{2,1,0:T(8,128)(2,1)S(1)} %copy-done.2, bf16[512,1024]{1,0:T(8,128)(2,1)S(1)} %bitcast.12, ...), custom_call_target="tpu_custom_call" | custom-call | flops 4294967296 | tf_op jit(solution)/shard_map/pallas_call | solution.py:201
  55.1 1.7 %collective-permute-done.3.low = bf16[1024,128]{1,0:T(8,128)(2,1)S(1)} collective-permute-done((bf16[1024,128]{1,0:T(8,128)(2,1)S(1)}, bf16[1024,128]{1,0:T(8,128)(2,1)S(1)}, u32[]{:S(2)}, u32[]{:S(2)}) %collective-permute-start.3) | collective-permute-done | bytes 262176 | tf_op jit(solution)/shard_map/ppermute | solution.py:273
  56.9 0.0 collective-permute-done.4.high
  56.9 0.1 shard_map.52
  57.0 16.8 %all_to_all.10.parts = bf16[32,64,128]{2,1,0:T(8,128)(2,1)S(1)} all-to-all(bf16[32,64,128]{2,1,0:T(8,128)(2,1)S(1)} %bitcast.13), channel_id=1, replica_groups={{6,7,14,15,2,3,10,11,4,5,12,13,0,1,8,9,70,71,78,79,66,67,74,75,68,69,76..., dimensions={0} | all-to-all | bytes 1048576 | tf_op jit(solution)/shard_map/all_to_all | solution.py:279
  73.8 0.7 shard_map.53
  (1 shorter events, 0.0 us)
Async XLA Ops:
  0.0 13.5 %copy-start.4 = (s32[8]{0:T(128)S(1)}, s32[8]{0:T(128)}, u32[]{:S(2)}) copy-start(s32[8]{0:T(128)} %sizes.1) | copy-start | bytes 100
  0.0 13.5 %copy-start.3 = (s32[4,8,8]{2,1,0:T(8,128)S(1)}, s32[4,8,8]{2,1,0:T(8,128)}, u32[]{:S(2)}) copy-start(s32[4,8,8]{2,1,0:T(8,128)} %pattern.1) | copy-start | bytes 3076
  1.9 30.2 %all-to-all-start = ((bf16[64,8,1024]{2,1,0:T(8,128)(2,1)}), bf16[64,8,1024]{2,1,0:T(8,128)(2,1)S(1)}, u32[]{:S(2)}, u32[]{:S(2)}) async-start(bf16[64,8,1024]{2,1,0:T(8,128)(2,1)} %broadcast_in_dim.8), calls=%async_computation | async-start | bytes 2097152 | tf_op jit(solution)/shard_map/all_to_all | solution.py:267
  32.2 2.7 %copy-start = (bf16[4,512,512]{2,1,0:T(8,128)(2,1)S(1)}, bf16[4,512,512]{2,1,0:T(8,128)(2,1)}, u32[]{:S(2)}) copy-start(bf16[4,512,512]{2,1,0:T(8,128)(2,1)} %get-tuple-element.21.send_other) | copy-start | bytes 6291460
  32.2 2.7 %copy-start.1 = (bf16[4,512,512]{2,1,0:T(8,128)(2,1)S(1)}, bf16[4,512,512]{2,1,0:T(8,128)(2,1)}, u32[]{:S(2)}) copy-start(bf16[4,512,512]{2,1,0:T(8,128)(2,1)} %get-tuple-element.22.keep_own) | copy-start | bytes 6291460
  32.2 2.9 %copy-start.2 = (bf16[4,512,512]{2,1,0:T(8,128)(2,1)S(1)}, bf16[4,512,512]{2,1,0:T(8,128)(2,1)}, u32[]{:S(2)}) copy-start(bf16[4,512,512]{2,1,0:T(8,128)(2,1)} %get-tuple-element.23.keep_other) | copy-start | bytes 6291460
  32.2 2.7 %collective-permute-start = (bf16[512,1024]{1,0:T(8,128)(2,1)S(1)}, bf16[512,1024]{1,0:T(8,128)(2,1)S(1)}, u32[]{:S(2)}, u32[]{:S(2)}) collective-permute-start(bf16[512,1024]{1,0:T(8,128)(2,1)S(1)} %bitcast.9), channel_id=1, source_target_pairs={{0,16},{16,0},{1,17},{17,1},{2,18},{18,2},{3,19},{19,3},{4,20},{20... | collective-permute-start | bytes 3145736 | tf_op jit(solution)/shard_map/ppermute | solution.py:262
  38.4 4.3 %collective-permute-start.2 = (f32[2,1024,128]{2,1,0:T(8,128)S(1)}, f32[2,1024,128]{2,1,0:T(8,128)S(1)}, u32[]{:S(2)}, u32[]{:S(2)}) collective-permute-start(f32[2,1024,128]{2,1,0:T(8,128)S(1)} %shard_map.50), channel_id=1, source_target_pairs={{0,16},{16,0},{1,17},{17,1},{2,18},{18,2},{3,19},{19,3},{4,20},{20... | collective-permute-start | bytes 3145736 | tf_op jit(solution)/shard_map/ppermute | solution.py:262
  42.0 8.6 %collective-permute-start.1 = (f32[2,1024,128]{2,1,0:T(8,128)S(1)}, f32[2,1024,128]{2,1,0:T(8,128)S(1)}, u32[]{:S(2)}, u32[]{:S(2)}) collective-permute-start(f32[2,1024,128]{2,1,0:T(8,128)S(1)} %shard_map.48), channel_id=1, source_target_pairs={{0,16},{16,0},{1,17},{17,1},{2,18},{18,2},{3,19},{19,3},{4,20},{20... | collective-permute-start | bytes 3145736 | tf_op jit(solution)/shard_map/ppermute | solution.py:262
  47.3 9.5 %collective-permute-start.3 = (bf16[1024,128]{1,0:T(8,128)(2,1)S(1)}, bf16[1024,128]{1,0:T(8,128)(2,1)S(1)}, u32[]{:S(2)}, u32[]{:S(2)}) collective-permute-start(bf16[1024,128]{1,0:T(8,128)(2,1)S(1)} %get-tuple-element.25), channel_id=1, source_target_pairs={{0,32},{32,64},{64,96},{96,0},{1,33},{33,65},{65,97},{97,1},{2,34}... | collective-permute-start | bytes 786440 | tf_op jit(solution)/shard_map/ppermute | solution.py:273
  47.7 9.2 %collective-permute-start.4 = (bf16[1024,128]{1,0:T(8,128)(2,1)S(1)}, bf16[1024,128]{1,0:T(8,128)(2,1)S(1)}, u32[]{:S(2)}, u32[]{:S(2)}) collective-permute-start(bf16[1024,128]{1,0:T(8,128)(2,1)S(1)} %get-tuple-element.26), channel_id=1, source_target_pairs={{0,96},{32,0},{64,32},{96,64},{1,97},{33,1},{65,33},{97,65},{2,98}... | collective-permute-start | bytes 786440 | tf_op jit(solution)/shard_map/ppermute | solution.py:274
